TPU v7x, 32 devices: a whole 2x2x4 slice. The times are simulated.
32 devices in a mesh: group: 2 (over y), replica: 8 (over z, x), tensor: 2 (over core).
Axes of the slice: x: 2, y: 2, z: 4, core: 2. Of those that a mesh axis runs over, the one named last changes fastest.
Arguments:
- queries: bfloat16 [4096, 4096], P(('group', 'replica'), 'tensor'), parts along dimension 0, may hold values from -12 to 12
- keys: bfloat16 [4096, 512], P(('group', 'replica'), 'tensor'), parts along dimension 0, may hold values from -6 to 6
- values: bfloat16 [4096, 512], P(('group', 'replica'), 'tensor'), parts along dimension 0, may hold values from -6 to 6
- lengths: int32 [16], P('group'), parts along dimension 0, may hold values from 1 to 8, as said below
- slot_prompt: int32 [16, 2], P('group'), parts along dimension 0, may hold values from 0 to 7, as said below
- slot_span: int32 [16, 2], P('group'), parts along dimension 0, may hold values from 0 to 7
Outputs:
- attention: bfloat16 [16384, 4096], P(('group', 'replica'), 'tensor'), parts along dimension 0
- cache_keys: bfloat16 [16384, 512], P(('group', 'replica'), 'tensor'), parts along dimension 0
- cache_values: bfloat16 [16384, 512], P(('group', 'replica'), 'tensor'), parts along dimension 0
There are 2 independent parts, one for each index of `group`. A program takes and returns all parts, laid end to end along the dimension named above; each array names one. Nothing has to cross between parts.
Inputs may be any that keep to these rules, and one draw needn't show every extreme that they name: The lengths sum to 16, and some prompt has exactly 8 spans. Every slot holds one span: each pair of a prompt p and a span m < lengths[p] is named by exactly one slot through slot_prompt and slot_span, and no other pair is named. Span m < min(lengths[p], 2) of prompt p sits in slot m of replica p.
All inputs are finite; a program needn't handle non-finite values.
Results may differ from a plain program's by a relative error of at most 0.0047.
Values may be sent and summed in bfloat16 or wider, within the bound.
No kernel may reach another device: no remote copies, remote signals or barrier semaphores. Data moves between devices by JAX's collectives and lax.ppermute only.
A program may use at most 128 MiB of HBM per device.

v0:
```python
import functools
import math

import jax
import jax.numpy as jnp
from jax import lax
from jax.experimental import pallas as pl
from jax.experimental.pallas import tpu as pltpu
from jax.sharding import PartitionSpec as P

HDIM = 128
SPAN = 128
SLOTS = 2
MAXC = 8
BLOCK = 4
PART = 2
LOG2E = 1.0 / math.log(2.0)
VMEM_BYTES = 40 * 1024 * 1024
MOST_VMEM_BYTES = 60 * 1024 * 1024
LEAST_SUM, MOST_SUM = 1e-20, 1e30
ANY = pl.BlockSpec(memory_space=pl.ANY)
SMEM = pl.BlockSpec(memory_space=pltpu.SMEM)
VMEM = pl.BlockSpec(memory_space=pltpu.VMEM)


def cost_of(us):
    return pl.CostEstimate(flops=int(us * 1.15e9), bytes_accessed=0, transcendentals=0)


def column_ring(replicas):
    return list(range(0, replicas, 2)) + list(range(replicas - 1, 0, -2))


def copy_all(copies):
    for copy in copies:
        copy.start()
    for copy in copies:
        copy.wait()


def pack_kv_kernel(k_ref, v_ref, o_ref, sems):
    copy_all(
        [
            pltpu.make_async_copy(k_ref.at[SPAN:], o_ref.at[:SPAN], sems.at[0]),
            pltpu.make_async_copy(v_ref.at[SPAN:], o_ref.at[SPAN:], sems.at[1]),
        ]
    )


def pack_kv(keys, values):
    return pl.pallas_call(
        pack_kv_kernel,
        out_shape=jax.ShapeDtypeStruct((2 * SPAN, keys.shape[1]), keys.dtype),
        in_specs=[ANY] * 2,
        out_specs=VMEM,
        scratch_shapes=[pltpu.SemaphoreType.DMA((2,))],
        compiler_params=pltpu.CompilerParams(vmem_limit_bytes=MOST_VMEM_BYTES),
        cost_estimate=cost_of(1),
    )(keys, values)


def pack_q_kernel(q_ref, o_top, o_bottom, sems):
    half = SPAN // 2
    copy_all(
        [
            pltpu.make_async_copy(q_ref.at[SPAN : SPAN + half], o_top, sems.at[0]),
            pltpu.make_async_copy(q_ref.at[SPAN + half :], o_bottom, sems.at[1]),
        ]
    )


def pack_q(queries):
    half = jax.ShapeDtypeStruct((SPAN // 2, queries.shape[1]), queries.dtype)
    return pl.pallas_call(
        pack_q_kernel,
        out_shape=(half, half),
        in_specs=[ANY],
        out_specs=(VMEM, VMEM),
        scratch_shapes=[pltpu.SemaphoreType.DMA((2,))],
        compiler_params=pltpu.CompilerParams(vmem_limit_bytes=VMEM_BYTES),
        cost_estimate=cost_of(1),
    )(queries)


def places(lengths, slot_prompt, slot_span):
    replicas = lengths.shape[0]
    mine = lax.axis_index("replica")
    ring = jnp.arange(replicas, dtype=jnp.int32)
    place = jnp.where(mine % 2 == 0, mine // 2, replicas - 1 - mine // 2)
    at = (place + replicas - ring) % replicas
    other = jnp.where(at < replicas // 2, 2 * at, 2 * (replicas - at) - 1)
    chosen = other[:, None] == ring[None, :]
    wanted = chosen & (slot_prompt[None, :, 1] == mine) & (ring[:, None] > 0)
    spans = jnp.where(wanted, slot_span[None, :, 1] + 1, 0)
    whole = jnp.where(chosen & (ring[:, None] == 0), lengths[None, :] + 1, 0)
    return jnp.sum(spans + whole, axis=1) - 1


def widen(v_ref, wide_ref):
    for at in range(0, v_ref.shape[-1], HDIM):
        wide_ref[:, 2 * at : 2 * at + HDIM] = v_ref[:, at : at + HDIM]
        wide_ref[:, 2 * at + HDIM : 2 * at + 2 * HDIM] = jnp.ones(
            (v_ref.shape[0], HDIM), v_ref.dtype
        )


def stack(q_ref, stacked):
    kv_heads, rows, _ = stacked.shape
    tall = q_ref.shape[0]
    group = rows // tall
    for shared in range(kv_heads):
        for h in range(group):
            at = (shared * group + h) * HDIM
            stacked[shared, h * tall : (h + 1) * tall, :] = q_ref[:, at : at + HDIM]


def divide(mixed, shared, o_ref, bounds):
    tall = o_ref.shape[0]
    group = mixed.shape[0] // tall
    total = mixed[:, HDIM:]
    inverse = pl.reciprocal(total, approx=True)
    inverse = inverse * (2.0 - total * inverse)
    result = (mixed[:, :HDIM] * inverse).astype(o_ref.dtype)
    for h in range(group):
        at = (shared * group + h) * HDIM
        o_ref[:, at : at + HDIM] = result[h * tall : (h + 1) * tall, :]
    total = total.reshape(-1, 8, HDIM)
    bounds[0] = jnp.minimum(bounds[0], jnp.min(total, axis=0))
    bounds[1] = jnp.maximum(bounds[1], jnp.max(total, axis=0))


def attend_piece(span, start, stacked, k_ref, wide_ref, mixed, o_ref, bounds):
    kv_heads, rows, _ = stacked.shape
    heads = range(kv_heads)
    tall = o_ref.shape[0]
    scale = LOG2E / math.sqrt(HDIM)
    blocks = span // BLOCK
    edge = span % PART * SPAN + start

    def keys_of(block, spans):
        return pl.ds(pl.multiple_of(block * BLOCK * SPAN, BLOCK * SPAN), spans * SPAN)

    def scores(shared, block, spans, masked):
        found = lax.dot_general(
            stacked[shared],
            k_ref[keys_of(block, spans), shared * HDIM : (shared + 1) * HDIM],
            (((1,), (1,)), ((), ())),
            preferred_element_type=jnp.float32,
        )
        if masked:
            seen = (spans - PART) * SPAN
            row = lax.broadcasted_iota(jnp.int32, (rows, PART * SPAN), 0) % tall
            column = lax.broadcasted_iota(jnp.int32, (rows, PART * SPAN), 1)
            last = jnp.where(column <= row + edge, found[:, seen:], -jnp.inf)
            found = jnp.concatenate([found[:, :seen], last], axis=1) if seen else last
        return found

    def products(shared, block, spans, found):
        return jnp.dot(
            jnp.exp2(found * scale).astype(jnp.bfloat16),
            wide_ref[keys_of(block, spans), 2 * shared * HDIM : 2 * (shared + 1) * HDIM],
            preferred_element_type=jnp.float32,
        )

    def add(block, carry):
        found = [scores(shared, block, BLOCK, False) for shared in heads]
        for shared in heads:
            mixed[shared] += products(shared, block, BLOCK, found[shared])
        return carry

    mixed[...] = jnp.zeros_like(mixed)
    most = k_ref.shape[0] // SPAN
    if most > BLOCK:
        lax.fori_loop(0, blocks, add, 0)
    for spans in range(PART, min(BLOCK, most) + 1, PART):

        @pl.when(span % BLOCK // PART == spans // PART - 1)
        def _(spans=spans):
            found = [scores(shared, blocks, spans, True) for shared in heads]
            for shared in heads:
                whole = mixed[shared] + products(shared, blocks, spans, found[shared])
                divide(whole, shared, o_ref, bounds)


def attend_piece_shifted(span, start, stacked, k_ref, wide_ref, mixed, o_ref, bounds, top):
    kv_heads, rows, _ = stacked.shape
    tall = o_ref.shape[0]
    scale = LOG2E / math.sqrt(HDIM)

    def one_head(shared, carry):
        def scores(block):
            found = lax.dot_general(
                stacked[shared],
                k_ref[rows_of(block), pl.ds(pl.multiple_of(shared * HDIM, HDIM), HDIM)],
                (((1,), (1,)), ((), ())),
                preferred_element_type=jnp.float32,
            )
            row = lax.broadcasted_iota(jnp.int32, (rows, SPAN), 0) % tall
            column = lax.broadcasted_iota(jnp.int32, (rows, SPAN), 1)
            return jnp.where(column <= row + (span - block) * SPAN + start, found, -jnp.inf)

        def look(block, carry):
            top[...] = jnp.maximum(top[...], scores(block))
            return carry

        def add(block, carry):
            weights = jnp.exp2((scores(block) - top[...]) * scale).astype(jnp.bfloat16)
            mixed[shared] += jnp.dot(
                weights,
                wide_ref[
                    rows_of(block), pl.ds(pl.multiple_of(2 * shared * HDIM, 2 * HDIM), 2 * HDIM)
                ],
                preferred_element_type=jnp.float32,
            )
            return carry

        top[...] = jnp.full_like(top, -jnp.inf)
        lax.fori_loop(0, span + 1, look, 0)
        top[...] = jnp.broadcast_to(jnp.max(top[...], axis=1, keepdims=True), top.shape)
        mixed[shared] = jnp.zeros(mixed.shape[1:], mixed.dtype)
        lax.fori_loop(0, span + 1, add, 0)
        return carry

    lax.fori_loop(0, kv_heads, one_head, 0)
    for shared in range(kv_heads):
        divide(mixed[shared], shared, o_ref, bounds)


def twice_if_needed(work, drain, bounds):
    bounds[...] = jnp.ones_like(bounds)
    work(False)
    safe = (jnp.min(bounds[0]) > LEAST_SUM) & (jnp.max(bounds[1]) < MOST_SUM)
    drain()

    @pl.when(jnp.logical_not(safe))
    def _():
        work(True)
        drain()


def work_space(count, tall, width, key_width):
    kv_heads = key_width // HDIM
    rows = width // key_width * tall
    return [
        pltpu.VMEM((count, kv_heads, rows, HDIM), jnp.bfloat16),
        pltpu.VMEM((kv_heads, rows, 2 * HDIM), jnp.float32),
        pltpu.VMEM((rows, HDIM), jnp.float32),
        pltpu.VMEM((2, 8, HDIM), jnp.float32),
    ]


def rows_of(span):
    return pl.ds(pl.multiple_of(span * SPAN, SPAN), SPAN)


def half_of(span, start):
    return pl.ds(pl.multiple_of(span * SPAN + start, SPAN // 2), SPAN // 2)


def pick(j, options):
    chosen = options[0]
    for n in range(1, len(options)):
        chosen = jnp.where(j == n, options[n], chosen)
    return chosen


def attend_pieces(dests, starts, q_refs, k_ref, wide_ref, out_buf, store, stacked, mixed, top, bounds):
    count = len(dests)
    for j in range(count):

        @pl.when(dests[j] >= 0)
        def _(j=j):
            stack(q_refs[j], stacked.at[j])

    def work(shifted):
        def one(j, carry):
            dest, start = pick(j, dests), pick(j, starts)

            @pl.when(dest >= 0)
            def _():
                args = (dest, start, stacked.at[j], k_ref, wide_ref, mixed, out_buf.at[j], bounds)
                if shifted:
                    attend_piece_shifted(*args, top)
                else:
                    attend_piece(*args)
                if store is not None:
                    store(j, dest, start).start()

            return carry

        lax.fori_loop(0, count, one, 0)

    def drain():
        if store is not None:
            for j in range(count):
                pl.when(dests[j] >= 0)(store(j, jnp.maximum(dests[j], 0), starts[j]).wait)

    twice_if_needed(work, drain, bounds)


def stores(buf, o_ref, sems):
    return lambda j, span, start: pltpu.make_async_copy(
        buf.at[j], o_ref.at[half_of(span, start)], sems.at[j]
    )


def local_kernel(length_ref, q_hbm, k_hbm, v_hbm, out_buf, q_ref, k_ref, v_ref, wide, sems, *work):
    live = length_ref[lax.axis_index("replica")]

    def fetch(slot):
        rows = slice(slot * SPAN, (slot + 1) * SPAN)
        return pltpu.make_async_copy(q_hbm.at[rows], q_ref.at[rows], sems.at[2 + slot])

    fetches = [
        pltpu.make_async_copy(k_hbm, k_ref, sems.at[0]),
        pltpu.make_async_copy(v_hbm, v_ref, sems.at[1]),
        fetch(0),
    ]
    for copy in fetches:
        copy.start()
    pl.when(live > 1)(fetch(1).start)
    for copy in fetches:
        copy.wait()
    widen(v_ref, wide)
    pl.when(live > 1)(fetch(1).wait)
    half = SPAN // 2
    second = jnp.where(live > 1, 1, -1)
    attend_pieces(
        [jnp.int32(0), jnp.int32(0), second, second],
        [0, half, 0, half],
        [q_ref.at[n * half : (n + 1) * half] for n in range(2 * SLOTS)],
        k_ref,
        wide,
        out_buf,
        None,
        *work,
    )


def attend_local(lengths, queries, keys, values):
    width, key_width = queries.shape[1], keys.shape[1]
    return pl.pallas_call(
        local_kernel,
        out_shape=jax.ShapeDtypeStruct((2 * SLOTS, SPAN // 2, width), queries.dtype),
        in_specs=[SMEM, ANY, ANY, ANY],
        out_specs=VMEM,
        scratch_shapes=[
            pltpu.VMEM(queries.shape, queries.dtype),
            pltpu.VMEM(keys.shape, keys.dtype),
            pltpu.VMEM(values.shape, values.dtype),
            pltpu.VMEM((SLOTS * SPAN, 2 * key_width), keys.dtype),
            pltpu.SemaphoreType.DMA((2 + SLOTS,)),
            *work_space(2 * SLOTS, SPAN // 2, width, key_width),
        ],
        compiler_params=pltpu.CompilerParams(vmem_limit_bytes=VMEM_BYTES),
        cost_estimate=cost_of(3.5),
    )(lengths, queries, keys, values)


def any_of(dests):
    return functools.reduce(jnp.maximum, dests) >= 0


def first_kernel(kv_offsets, places, meta_ref, own_k, own_v, *refs):
    blocks, refs = refs[: len(kv_offsets)], refs[len(kv_offsets) :]
    q_refs, refs = refs[: len(places)], refs[len(places) :]
    local, o_k, o_v, k_buf, wide, out_buf, o_ref, v_buf, zeros, in_sems, out_sems, span_sems, *work = refs
    live = meta_ref[0]
    half = SPAN // 2

    def fetches():
        yield None, own_k.at[:SPAN], k_buf.at[rows_of(0)]
        yield None, own_v.at[:SPAN], v_buf.at[rows_of(0)]
        yield live > 1, own_k.at[SPAN:], k_buf.at[rows_of(1)]
        yield live > 1, own_v.at[SPAN:], v_buf.at[rows_of(1)]

    def each(act):
        for n, (needed, here, there) in enumerate(fetches()):
            copy = getattr(pltpu.make_async_copy(here, there, in_sems.at[n]), act)
            if needed is None:
                copy()
            else:
                pl.when(needed)(copy)

    def each_span(act):
        for span in range(MAXC):
            if span < SLOTS:
                for n in range(2):
                    copy = pltpu.make_async_copy(
                        local.at[2 * span + n],
                        o_ref.at[half_of(span, n * half)],
                        span_sems.at[span, n],
                    )
                    pl.when(span < live)(getattr(copy, act))
            if span > 0:
                copy = pltpu.make_async_copy(zeros, o_ref.at[rows_of(span)], span_sems.at[span, 0])
                pl.when(span >= live)(getattr(copy, act))

    each("start")
    zeros[...] = jnp.zeros_like(zeros)
    each_span("start")
    for span in range(1, MAXC):

        @pl.when(span >= live)
        def _(span=span):
            k_buf[rows_of(span), :] = jnp.zeros((SPAN, k_buf.shape[1]), k_buf.dtype)
            v_buf[rows_of(span), :] = jnp.zeros((SPAN, v_buf.shape[1]), v_buf.dtype)

    for block, offset in zip(blocks, kv_offsets, strict=True):
        dest = meta_ref[offset]

        @pl.when(dest >= 0)
        def _(block=block, dest=dest):
            k_buf[rows_of(dest), :] = block[:SPAN, :]
            v_buf[rows_of(dest), :] = block[SPAN:, :]

    each("wait")
    copy_k = pltpu.make_async_copy(k_buf, o_k, out_sems.at[0])
    copy_v = pltpu.make_async_copy(v_buf, o_v, out_sems.at[1])
    copy_k.start()
    copy_v.start()
    dests = [meta_ref[offset] for offset, _ in places]

    @pl.when(live > 1)
    def _():
        widen(v_buf, wide)

    @pl.when(any_of(dests))
    def _():
        starts = [start for _, start in places]
        attend_pieces(dests, starts, q_refs, k_buf, wide, out_buf, None, *work)

    copy_k.wait()
    copy_v.wait()
    each_span("wait")


def attend_first(meta, keys, values, kv_offsets, kv_blocks, pieces, local):
    rows, key_width = MAXC * SPAN, keys.shape[1]
    queries = [piece[0] for piece in pieces]
    places = [piece[1:] for piece in pieces]
    count, (tall, width) = len(pieces), queries[0].shape
    out = jax.ShapeDtypeStruct((rows, key_width), keys.dtype)
    return pl.pallas_call(
        lambda *refs: first_kernel(kv_offsets, places, *refs),
        out_shape=(
            out,
            out,
            out,
            jax.ShapeDtypeStruct((rows, 2 * key_width), keys.dtype),
            jax.ShapeDtypeStruct((count, tall, width), keys.dtype),
            jax.ShapeDtypeStruct((rows, width), keys.dtype),
        ),
        in_specs=[SMEM, ANY, ANY] + [VMEM] * (len(kv_blocks) + count + 1),
        out_specs=(ANY, ANY, VMEM, VMEM, VMEM, ANY),
        scratch_shapes=[
            pltpu.VMEM((rows, key_width), keys.dtype),
            pltpu.VMEM((SPAN, width), keys.dtype),
            pltpu.SemaphoreType.DMA((4,)),
            pltpu.SemaphoreType.DMA((2,)),
            pltpu.SemaphoreType.DMA((MAXC, 2)),
            *work_space(count, tall, width, key_width),
        ],
        compiler_params=pltpu.CompilerParams(vmem_limit_bytes=VMEM_BYTES),
        cost_estimate=cost_of(2 + 1.3 * count),
    )(meta, keys, values, *kv_blocks, *queries, local)


def later_kernel(places, meta_ref, *refs):
    q_refs, (k_ref, wide_ref, out_buf, *work) = refs[: len(places)], refs[len(places) :]
    dests = [meta_ref[offset] for offset, _ in places]

    @pl.when(any_of(dests))
    def _():
        starts = [start for _, start in places]
        attend_pieces(dests, starts, q_refs, k_ref, wide_ref, out_buf, None, *work)


def attend_later(meta, pieces, ordered_keys, wide_values):
    queries = [piece[0] for piece in pieces]
    places = [piece[1:] for piece in pieces]
    count, (tall, width) = len(pieces), queries[0].shape
    return pl.pallas_call(
        lambda *refs: later_kernel(places, *refs),
        out_shape=jax.ShapeDtypeStruct((count, tall, width), ordered_keys.dtype),
        in_specs=[SMEM] + [VMEM] * (count + 2),
        out_specs=VMEM,
        scratch_shapes=work_space(count, tall, width, ordered_keys.shape[1]),
        compiler_params=pltpu.CompilerParams(vmem_limit_bytes=VMEM_BYTES),
        cost_estimate=cost_of(1 + 1.3 * count),
    )(meta, *queries, ordered_keys, wide_values)


def last_kernel(before, places, meta_ref, *refs):
    results, refs = refs[: len(before)], refs[len(before) :]
    q_refs, refs = refs[: len(places)], refs[len(places) :]
    k_ref, wide_ref, _, o_ref, out_buf, sems, out_sems, *work = refs

    def each(act):
        for n, (result, its_places) in enumerate(zip(results, before, strict=True)):
            for j, (offset, start) in enumerate(its_places):
                dest = meta_ref[offset]
                copy = pltpu.make_async_copy(
                    result.at[j], o_ref.at[half_of(jnp.maximum(dest, 0), start)], sems.at[n, j]
                )
                pl.when(dest >= 0)(getattr(copy, act))

    each("start")
    dests = [meta_ref[offset] for offset, _ in places]

    @pl.when(any_of(dests))
    def _():
        starts = [start for _, start in places]
        store = stores(out_buf, o_ref, out_sems)
        attend_pieces(dests, starts, q_refs, k_ref, wide_ref, out_buf, store, *work)

    each("wait")


def attend_last(meta, before, results, pieces, ordered_keys, wide_values, attention):
    queries = [piece[0] for piece in pieces]
    places = [piece[1:] for piece in pieces]
    count, (tall, width) = len(pieces), queries[0].shape
    most = max(len(its_places) for its_places in before)
    return pl.pallas_call(
        lambda *refs: last_kernel(before, places, *refs),
        out_shape=jax.ShapeDtypeStruct(attention.shape, attention.dtype),
        in_specs=[SMEM] + [VMEM] * (len(results) + count + 2) + [ANY],
        out_specs=ANY,
        input_output_aliases={len(results) + count + 3: 0},
        scratch_shapes=[
            pltpu.VMEM((count, tall, width), attention.dtype),
            pltpu.SemaphoreType.DMA((len(before), most)),
            pltpu.SemaphoreType.DMA((count,)),
            *work_space(count, tall, width, ordered_keys.shape[1]),
        ],
        compiler_params=pltpu.CompilerParams(vmem_limit_bytes=VMEM_BYTES),
        cost_estimate=cost_of(4),
    )(meta, *results, *queries, ordered_keys, wide_values, attention)


def gathered_kernel(meta_ref, first_ref, later_ref, k_ref, v_ref, o_ref, wide, stacked, mixed, top, bounds):
    at = pl.program_id(1)
    live = meta_ref[0]
    widen(v_ref, wide)

    @pl.when(at == 0)
    def _():
        stack(first_ref, stacked.at[0])

    @pl.when(at > 0)
    def _():
        stack(later_ref.at[0], stacked.at[0])

    def work(shifted):
        args = (at, 0, stacked.at[0], k_ref, wide, mixed, o_ref, bounds)
        if shifted:
            attend_piece_shifted(*args, top)
        else:
            attend_piece(*args)

    @pl.when(at < live)
    def _():
        twice_if_needed(work, lambda: None, bounds)

    @pl.when(at >= live)
    def _():
        o_ref[...] = jnp.zeros_like(o_ref)


def attend_gathered(live, source, first, later, cache_keys, cache_values):
    home_rows, key_width = cache_keys.shape
    width = first.shape[1]
    groups = key_width // HDIM
    part = width // groups
    meta = jnp.concatenate([live.reshape(1), source]).astype(jnp.int32)
    return pl.pallas_call(
        gathered_kernel,
        out_shape=jax.ShapeDtypeStruct((home_rows, width), first.dtype),
        grid_spec=pltpu.PrefetchScalarGridSpec(
            num_scalar_prefetch=1,
            grid=(groups, MAXC),
            in_specs=[
                pl.BlockSpec((SPAN, part), lambda g, m, meta: (0, g)),
                pl.BlockSpec((1, SPAN, part), lambda g, m, meta: (meta[1 + m], 0, g)),
                pl.BlockSpec((home_rows, HDIM), lambda g, m, meta: (0, g)),
                pl.BlockSpec((home_rows, HDIM), lambda g, m, meta: (0, g)),
            ],
            out_specs=pl.BlockSpec((SPAN, part), lambda g, m, meta: (m, g)),
            scratch_shapes=[
                pltpu.VMEM((home_rows, 2 * HDIM), cache_keys.dtype),
                *work_space(1, SPAN, part, HDIM),
            ],
        ),
        compiler_params=pltpu.CompilerParams(vmem_limit_bytes=VMEM_BYTES),
    )(meta, first, later, cache_keys, cache_values)


def gather_all(queries, keys, values, lengths, slot_prompt, slot_span):
    mine = lax.axis_index("replica")
    home_rows, key_width = MAXC * SPAN, keys.shape[1]
    live = lengths[mine]
    spans = jnp.arange(MAXC, dtype=jnp.int32)
    matches = (slot_prompt[None, :, 1] == mine) & (slot_span[None, :, 1] == spans[:, None])
    here = jnp.any(matches, axis=1)
    source = jnp.argmax(matches, axis=1).astype(jnp.int32)
    slots_k = lax.all_gather(keys[SPAN:], "replica")
    slots_v = lax.all_gather(values[SPAN:], "replica")
    slots_q = lax.all_gather(queries[SPAN:], "replica")

    def in_order(first, slots):
        picked = jnp.take(slots, source, axis=0)
        kept = jnp.where(here[:, None, None], picked, jnp.zeros((), slots.dtype))
        return jnp.concatenate([first, kept[1:].reshape(home_rows - SPAN, key_width)], axis=0)

    cache_keys = in_order(keys[:SPAN], slots_k)
    cache_values = in_order(values[:SPAN], slots_v)
    attention = attend_gathered(live, source, queries[:SPAN], slots_q, cache_keys, cache_values)
    return (attention, cache_keys, cache_values)


def per_device(queries, keys, values, lengths, slot_prompt, slot_span):
    replicas = lax.axis_size("replica")
    if replicas != 8:
        return gather_all(queries, keys, values, lengths, slot_prompt, slot_span)
    ring = column_ring(replicas)
    farthest = replicas // 2

    def after(block, *others):
        return lax.optimization_barrier((block, others))[0]

    def joined(both):
        return list(lax.optimization_barrier(tuple(both)))

    def shift(block, step):
        pairs = [(r, ring[(n + step) % replicas]) for n, r in enumerate(ring)]
        return lax.ppermute(block, "replica", pairs)

    def go_on(both):
        return [shift(both[0], 1), shift(both[1], -1)]

    own_kv = pack_kv(keys, values)
    kv = [[own_kv, own_kv]]
    kv.append(go_on(kv[0]))
    own_top, own_bottom = pack_q(after(queries, own_kv))
    first, second = [[own_top, own_bottom]], [[own_bottom, own_top]]
    first.append(joined(go_on(first[0])))
    kv[1] = joined(kv[1])
    kv.append(joined(go_on(kv[1])))
    local = attend_local(lengths, after(queries, kv[1]), keys, values)
    second.append(joined(go_on([after(block, first[1]) for block in second[0]])))
    kv.append(joined(go_on([after(block, local) for block in kv[2]])))
    first.append(joined(go_on([after(block, kv[3]) for block in first[1]])))
    kv.append([shift(kv[3][0], 1)])
    second.append(joined(go_on([after(block, kv[3]) for block in second[1]])))
    meta = places(lengths, slot_prompt, slot_span)
    offsets = [[n, replicas - n] for n in range(1, farthest)]

    def wave(n, which):
        up, down = offsets[n - 1]
        if which is first:
            return [(first[n][0], up, 0), (first[n][1], down, half)]
        return [(second[n][0], up, half), (second[n][1], down, 0)]

    half = SPAN // 2
    cache_keys, cache_values, ordered_keys, wide_values, result, attention = attend_first(
        meta,
        keys,
        values,
        sum(offsets, []) + [farthest],
        sum(kv[1:], []),
        wave(1, first) + wave(1, second),
        local,
    )
    results, before = [result], [wave(1, first) + wave(1, second)]

    def attend(n, which):
        results.append(attend_later(meta, wave(n, which), ordered_keys, wide_values))
        before.append(wave(n, which))

    first.append(joined(go_on(first[2])))
    attend(2, first)
    second.append(joined(go_on([after(block, results[-1]) for block in second[2]])))
    attend(2, second)
    last = [
        (shift(after(first[3][0], results[-1]), 1), farthest, 0),
        (shift(after(first[3][1], results[-1]), -1), farthest, half),
    ]
    attend(3, first)
    attend(3, second)
    before = [[piece[1:] for piece in pieces] for pieces in before]
    attention = attend_last(
        meta, before, results, last, ordered_keys, wide_values, attention
    )
    return (attention, cache_keys, cache_values)


def solution(mesh):
    in_specs = (
        P(("group", "replica"), "tensor"),
        P(("group", "replica"), "tensor"),
        P(("group", "replica"), "tensor"),
        P("group"),
        P("group", None),
        P("group", None),
    )
    out_specs = (
        P(("group", "replica"), "tensor"),
        P(("group", "replica"), "tensor"),
        P(("group", "replica"), "tensor"),
    )
    return jax.shard_map(
        per_device, mesh=mesh, in_specs=in_specs, out_specs=out_specs, check_vma=False
    )
```

profile of v0, /device:TPU:10, one launch (start us, length us, event | category | flops | bytes accessed | tf_op | source)
XLA Modules:
  0.0 154.9 jit_solution(6977043333749718514)
XLA Ops:
  0.6 0.0 copy-start.3
  0.6 0.0 copy-start.2
  0.7 0.0 copy-start.1
  0.7 0.0 copy-start.4
  0.7 0.0 copy-start.5
  0.7 0.0 copy-start
  0.7 1.6 %shard_map.85 = bf16[256,256]{1,0:T(8,128)(2,1)} custom-call(bf16[256,256]{1,0:T(8,128)(2,1)} %refs_1_.1, bf16[256,256]{1,0:T(8,128)(2,1)} %refs_2_.1), custom_call_target="tpu_custom_call" | custom-call | flops 1150000000 | tf_op jit(solution)/shard_map/pallas_call | solution.py:51
  2.3 1.6 %collective-permute-start.1 = (bf16[256,256]{1,0:T(8,128)(2,1)}, bf16[256,256]{1,0:T(8,128)(2,1)S(1)}, u32[]{:S(2)}, u32[]{:S(2)}) collective-permute-start(bf16[256,256]{1,0:T(8,128)(2,1)} %shard_map.85), channel_id=1, source_target_pairs={{0,2},{4,0},{8,4},{12,8},{14,12},{10,14},{6,10},{2,6},{1,3},{5,1},... | collective-permute-start | bytes 393224 | tf_op jit(solution)/shard_map/ppermute | solution.py:637
  4.0 0.4 collective-permute-start
  4.4 0.0 copy-done.1
  4.4 0.1 shard_map.87
  4.5 0.5 collective-permute-start.7
  5.0 1.6 %collective-permute-start.8 = (bf16[64,2048]{1,0:T(8,128)(2,1)S(1)}, bf16[64,2048]{1,0:T(8,128)(2,1)S(1)}, u32[]{:S(2)}, u32[]{:S(2)}) collective-permute-start(bf16[64,2048]{1,0:T(8,128)(2,1)S(1)} %get-tuple-element.57), channel_id=1, source_target_pairs={{0,2},{4,0},{8,4},{12,8},{14,12},{10,14},{6,10},{2,6},{1,3},{5,1},... | collective-permute-start | bytes 786440 | tf_op jit(solution)/shard_map/ppermute | solution.py:637
  6.6 0.0 copy-done.4
  6.6 0.0 copy-done.5
  6.6 0.0 copy-done
  6.6 2.3 %collective-permute-done.1.refs_4_ = bf16[256,256]{1,0:T(8,128)(2,1)S(1)} collective-permute-done((bf16[256,256]{1,0:T(8,128)(2,1)}, bf16[256,256]{1,0:T(8,128)(2,1)S(1)}, u32[]{:S(2)}, u32[]{:S(2)}) %collective-permute-start.1) | collective-permute-done | bytes 131104 | tf_op jit(solution)/shard_map/ppermute | solution.py:637
  9.0 1.6 %collective-permute-done.refs_3_ = bf16[256,256]{1,0:T(8,128)(2,1)S(1)} collective-permute-done((bf16[256,256]{1,0:T(8,128)(2,1)}, bf16[256,256]{1,0:T(8,128)(2,1)S(1)}, u32[]{:S(2)}, u32[]{:S(2)}) %collective-permute-start) | collective-permute-done | bytes 131104 | tf_op jit(solution)/shard_map/ppermute | solution.py:637
  10.6 0.4 collective-permute-start.2
  11.1 1.6 %collective-permute-start.3 = (bf16[256,256]{1,0:T(8,128)(2,1)S(1)}, bf16[256,256]{1,0:T(8,128)(2,1)S(1)}, u32[]{:S(2)}, u32[]{:S(2)}) collective-permute-start(bf16[256,256]{1,0:T(8,128)(2,1)S(1)} %collective-permute-done.1.refs_4_), channel_id=1, source_target_pairs={{0,2},{4,0},{8,4},{12,8},{14,12},{10,14},{6,10},{2,6},{1,3},{5,1},... | collective-permute-start | bytes 393224 | tf_op jit(solution)/shard_map/ppermute | solution.py:637
  12.6 0.0 copy-done.3
  12.6 0.0 copy-done.2
  12.6 12.9 %shard_map.86.refs_14_ = bf16[4,64,2048]{2,1,0:T(8,128)(2,1)S(1)} custom-call(s32[8]{0:T(128)S(1)} %copy-done, bf16[256,2048]{1,0:T(8,128)(2,1)S(1)} %copy-done.1, bf16[256,256]{1,0:T(8,128)(2,1)S(1)} %copy-done.2, bf16[256,256]{1,0:T(8,128)(2,1)S(1)} %copy-done.3), custom_call_target="tpu_custom_call" | custom-call | flops 4024999936 | tf_op jit(solution)/shard_map/pallas_call | solution.py:342
  25.6 0.0 collective-permute-done.2.refs_5_
  25.6 0.0 collective-permute-done.3.refs_6_
  25.6 0.5 collective-permute-start.4
  26.1 1.6 %collective-permute-start.5 = (bf16[256,256]{1,0:T(8,128)(2,1)S(1)}, bf16[256,256]{1,0:T(8,128)(2,1)S(1)}, u32[]{:S(2)}, u32[]{:S(2)}) collective-permute-start(bf16[256,256]{1,0:T(8,128)(2,1)S(1)} %collective-permute-done.3.refs_6_), channel_id=1, source_target_pairs={{0,2},{4,0},{8,4},{12,8},{14,12},{10,14},{6,10},{2,6},{1,3},{5,1},... | collective-permute-start | bytes 393224 | tf_op jit(solution)/shard_map/ppermute | solution.py:637
  27.7 0.0 collective-permute-done.7.refs_10_
  27.7 0.0 collective-permute-done.8.refs_11_
  27.7 0.5 collective-permute-start.9
  28.2 1.6 %collective-permute-start.10 = (bf16[64,2048]{1,0:T(8,128)(2,1)S(1)}, bf16[64,2048]{1,0:T(8,128)(2,1)S(1)}, u32[]{:S(2)}, u32[]{:S(2)}) collective-permute-start(bf16[64,2048]{1,0:T(8,128)(2,1)S(1)} %get-tuple-element.58), channel_id=1, source_target_pairs={{0,2},{4,0},{8,4},{12,8},{14,12},{10,14},{6,10},{2,6},{1,3},{5,1},... | collective-permute-start | bytes 786440 | tf_op jit(solution)/shard_map/ppermute | solution.py:637
  29.8 0.2 add_reduce_fusion
  29.9 2.1 %collective-permute-done.4.refs_7_ = bf16[256,256]{1,0:T(8,128)(2,1)S(1)} collective-permute-done((bf16[256,256]{1,0:T(8,128)(2,1)S(1)}, bf16[256,256]{1,0:T(8,128)(2,1)S(1)}, u32[]{:S(2)}, u32[]{:S(2)}) %collective-permute-start.4) | collective-permute-done | bytes 131104 | tf_op jit(solution)/shard_map/ppermute | solution.py:637
  32.1 0.4 collective-permute-done.5.refs_8_
  32.5 0.1 collective-permute-start.6
  32.6 0.0 collective-permute-start.11
  32.6 2.0 %collective-permute-start.12 = (bf16[64,2048]{1,0:T(8,128)(2,1)S(1)}, bf16[64,2048]{1,0:T(8,128)(2,1)S(1)}, u32[]{:S(2)}, u32[]{:S(2)}) collective-permute-start(bf16[64,2048]{1,0:T(8,128)(2,1)S(1)} %collective-permute-done.8.refs_11_), channel_id=1, source_target_pairs={{0,2},{4,0},{8,4},{12,8},{14,12},{10,14},{6,10},{2,6},{1,3},{5,1},... | collective-permute-start | bytes 786440 | tf_op jit(solution)/shard_map/ppermute | solution.py:637
  34.6 3.1 %collective-permute-done.9.refs_12_ = bf16[64,2048]{1,0:T(8,128)(2,1)S(1)} collective-permute-done((bf16[64,2048]{1,0:T(8,128)(2,1)S(1)}, bf16[64,2048]{1,0:T(8,128)(2,1)S(1)}, u32[]{:S(2)}, u32[]{:S(2)}) %collective-permute-start.9) | collective-permute-done | bytes 262176 | tf_op jit(solution)/shard_map/ppermute | solution.py:637
  37.7 0.4 collective-permute-done.10.refs_13_
  38.1 0.1 collective-permute-start.13
  38.2 2.0 %collective-permute-start.14 = (bf16[64,2048]{1,0:T(8,128)(2,1)S(1)}, bf16[64,2048]{1,0:T(8,128)(2,1)S(1)}, u32[]{:S(2)}, u32[]{:S(2)}) collective-permute-start(bf16[64,2048]{1,0:T(8,128)(2,1)S(1)} %collective-permute-done.10.refs_13_), channel_id=1, source_target_pairs={{0,2},{4,0},{8,4},{12,8},{14,12},{10,14},{6,10},{2,6},{1,3},{5,1},... | collective-permute-start | bytes 786440 | tf_op jit(solution)/shard_map/ppermute | solution.py:637
  40.2 0.3 collective-permute-done.6.refs_9_
  40.5 11.8 %shard_map.88 = (bf16[1024,256]{1,0:T(8,128)(2,1)}, bf16[1024,256]{1,0:T(8,128)(2,1)}, bf16[1024,256]{1,0:T(8,128)(2,1)S(1)}, bf16[1024,512]{1,0:T(8,128)(2,1)S(...) custom-call(s32[8]{0:T(128)S(1)} %broadcast_add_fusion.1.refs_0_, bf16[256,256]{1,0:T(8,128)(2,1)S(1)} %copy-done.2, ...), custom_call_target="tpu_custom_call" | custom-call | flops 8280000000 | tf_op jit(solution)/shard_map/pallas_call | solution.py:444
  52.3 0.0 collective-permute-done.11.refs_1_
  52.3 0.0 collective-permute-done.12.refs_2_
  52.3 0.1 collective-permute-start.15
  52.4 2.0 %collective-permute-start.16 = (bf16[64,2048]{1,0:T(8,128)(2,1)S(1)}, bf16[64,2048]{1,0:T(8,128)(2,1)S(1)}, u32[]{:S(2)}, u32[]{:S(2)}) collective-permute-start(bf16[64,2048]{1,0:T(8,128)(2,1)S(1)} %collective-permute-done.12.refs_2_), channel_id=1, source_target_pairs={{0,2},{4,0},{8,4},{12,8},{14,12},{10,14},{6,10},{2,6},{1,3},{5,1},... | collective-permute-start | bytes 786440 | tf_op jit(solution)/shard_map/ppermute | solution.py:637
  54.4 18.7 %shard_map.89.refs_2_ = bf16[2,64,2048]{2,1,0:T(8,128)(2,1)S(1)} custom-call(s32[8]{0:T(128)S(1)} %broadcast_add_fusion.1.refs_0_, bf16[64,2048]{1,0:T(8,128)(2,1)S(1)} %collective-permute-done.11.refs_1_, bf16[64,2048]{1,0:T(8,128)(2,1)S(1)} %collective-permute-done.12.refs_2_, bf16[1024,256]{1,0:T(8,128)(2,1)S(1)} %get-tuple-element.66.refs_3_.refs_8_, ...), custom_call_target="tpu_custom_call" | custom-call | flops 4140000000 | tf_op jit(solution)/shard_map/pallas_call | solution.py:483
  73.1 0.0 collective-permute-done.13.refs_1_
  73.1 0.0 collective-permute-done.14.refs_2_
  73.1 0.1 collective-permute-start.17
  73.1 2.0 %collective-permute-start.18 = (bf16[64,2048]{1,0:T(8,128)(2,1)S(1)}, bf16[64,2048]{1,0:T(8,128)(2,1)S(1)}, u32[]{:S(2)}, u32[]{:S(2)}) collective-permute-start(bf16[64,2048]{1,0:T(8,128)(2,1)S(1)} %collective-permute-done.14.refs_2_), channel_id=1, source_target_pairs={{0,2},{4,0},{8,4},{12,8},{14,12},{10,14},{6,10},{2,6},{1,3},{5,1},... | collective-permute-start | bytes 786440 | tf_op jit(solution)/shard_map/ppermute | solution.py:637
  75.2 18.9 %shard_map.90.refs_3_ = bf16[2,64,2048]{2,1,0:T(8,128)(2,1)S(1)} custom-call(s32[8]{0:T(128)S(1)} %broadcast_add_fusion.1.refs_0_, bf16[64,2048]{1,0:T(8,128)(2,1)S(1)} %collective-permute-done.13.refs_1_, bf16[64,2048]{1,0:T(8,128)(2,1)S(1)} %collective-permute-done.14.refs_2_, bf16[1024,256]{1,0:T(8,128)(2,1)S(1)} %get-tuple-element.66.refs_3_.refs_8_, ...), custom_call_target="tpu_custom_call" | custom-call | flops 4140000000 | tf_op jit(solution)/shard_map/pallas_call | solution.py:483
  94.0 0.0 collective-permute-done.15.refs_1_
  94.0 0.0 collective-permute-done.16.refs_2_
  94.1 0.1 collective-permute-start.19
  94.1 2.0 %collective-permute-start.20 = (bf16[64,2048]{1,0:T(8,128)(2,1)S(1)}, bf16[64,2048]{1,0:T(8,128)(2,1)S(1)}, u32[]{:S(2)}, u32[]{:S(2)}) collective-permute-start(bf16[64,2048]{1,0:T(8,128)(2,1)S(1)} %collective-permute-done.16.refs_2_), channel_id=1, source_target_pairs={{0,2},{4,0},{8,4},{12,8},{14,12},{10,14},{6,10},{2,6},{1,3},{5,1},... | collective-permute-start | bytes 786440 | tf_op jit(solution)/shard_map/ppermute | solution.py:637
  96.1 20.3 %shard_map.91.refs_4_ = bf16[2,64,2048]{2,1,0:T(8,128)(2,1)S(1)} custom-call(s32[8]{0:T(128)S(1)} %broadcast_add_fusion.1.refs_0_, bf16[64,2048]{1,0:T(8,128)(2,1)S(1)} %collective-permute-done.15.refs_1_, bf16[64,2048]{1,0:T(8,128)(2,1)S(1)} %collective-permute-done.16.refs_2_, bf16[1024,256]{1,0:T(8,128)(2,1)S(1)} %get-tuple-element.66.refs_3_.refs_8_, ...), custom_call_target="tpu_custom_call" | custom-call | flops 4140000000 | tf_op jit(solution)/shard_map/pallas_call | solution.py:483
  116.4 0.0 collective-permute-done.17.refs_1_
  116.4 0.0 collective-permute-done.18.refs_2_
  116.5 20.3 %shard_map.92.refs_5_ = bf16[2,64,2048]{2,1,0:T(8,128)(2,1)S(1)} custom-call(s32[8]{0:T(128)S(1)} %broadcast_add_fusion.1.refs_0_, bf16[64,2048]{1,0:T(8,128)(2,1)S(1)} %collective-permute-done.17.refs_1_, bf16[64,2048]{1,0:T(8,128)(2,1)S(1)} %collective-permute-done.18.refs_2_, bf16[1024,256]{1,0:T(8,128)(2,1)S(1)} %get-tuple-element.66.refs_3_.refs_8_, ...), custom_call_target="tpu_custom_call" | custom-call | flops 4140000000 | tf_op jit(solution)/shard_map/pallas_call | solution.py:483
  136.8 0.0 collective-permute-done.19.refs_6_
  136.8 0.0 collective-permute-done.20.refs_7_
  136.8 17.9 %shard_map.93 = bf16[1024,2048]{1,0:T(8,128)(2,1)} custom-call(s32[8]{0:T(128)S(1)} %broadcast_add_fusion.1.refs_0_, bf16[4,64,2048]{2,1,0:T(8,128)(2,1)S(1)} %get-tuple-element.61.refs_1_, bf16[2,64,2048]{2,1,0:T(8,128)(2,1)S(1)} %shard_map.89.refs_2_, bf16[2,64,2048]{2,1,0:T(8,128)(2,1)S(1)} %shard_map.90.refs_3_, ...), custom_call_target="tpu_custom_call", output_to_operand_aliasing={{}: (10, {})} | custom-call | flops 4600000000 | tf_op jit(solution)/shard_map/pallas_call | solution.py:525
  (5 shorter events, 0.0 us)
Async XLA Ops:
  0.6 12.0 %copy-start.3 = (bf16[256,256]{1,0:T(8,128)(2,1)S(1)}, bf16[256,256]{1,0:T(8,128)(2,1)}, u32[]{:S(2)}) copy-start(bf16[256,256]{1,0:T(8,128)(2,1)} %refs_2_.1) | copy-start | bytes 393220
  0.6 12.0 %copy-start.2 = (bf16[256,256]{1,0:T(8,128)(2,1)S(1)}, bf16[256,256]{1,0:T(8,128)(2,1)}, u32[]{:S(2)}) copy-start(bf16[256,256]{1,0:T(8,128)(2,1)} %refs_1_.1) | copy-start | bytes 393220
  0.7 3.8 %copy-start.1 = (bf16[256,2048]{1,0:T(8,128)(2,1)S(1)}, bf16[256,2048]{1,0:T(8,128)(2,1)}, u32[]{:S(2)}) copy-start(bf16[256,2048]{1,0:T(8,128)(2,1)} %q_ref) | copy-start | bytes 3145732
  0.7 5.9 %copy-start.4 = (s32[8,2]{0,1:T(2,128)S(1)}, s32[8,2]{0,1:T(2,128)}, u32[]{:S(2)}) copy-start(s32[8,2]{0,1:T(2,128)} %param.10) | copy-start | bytes 196
  0.7 5.9 %copy-start.5 = (s32[8,2]{0,1:T(2,128)S(1)}, s32[8,2]{0,1:T(2,128)}, u32[]{:S(2)}) copy-start(s32[8,2]{0,1:T(2,128)} %param.11) | copy-start | bytes 196
  0.7 5.9 %copy-start = (s32[8]{0:T(128)S(1)}, s32[8]{0:T(128)}, u32[]{:S(2)}) copy-start(s32[8]{0:T(128)} %length_ref.1) | copy-start | bytes 100
  2.3 6.6 %collective-permute-start.1 = (bf16[256,256]{1,0:T(8,128)(2,1)}, bf16[256,256]{1,0:T(8,128)(2,1)S(1)}, u32[]{:S(2)}, u32[]{:S(2)}) collective-permute-start(bf16[256,256]{1,0:T(8,128)(2,1)} %shard_map.85), channel_id=1, source_target_pairs={{0,2},{4,0},{8,4},{12,8},{14,12},{10,14},{6,10},{2,6},{1,3},{5,1},... | collective-permute-start | bytes 393224 | tf_op jit(solution)/shard_map/ppermute | solution.py:637
  4.0 6.6 %collective-permute-start = (bf16[256,256]{1,0:T(8,128)(2,1)}, bf16[256,256]{1,0:T(8,128)(2,1)S(1)}, u32[]{:S(2)}, u32[]{:S(2)}) collective-permute-start(bf16[256,256]{1,0:T(8,128)(2,1)} %shard_map.85), channel_id=1, source_target_pairs={{0,4},{4,8},{8,12},{12,14},{14,10},{10,6},{6,2},{2,0},{1,5},{5,9},... | collective-permute-start | bytes 393224 | tf_op jit(solution)/shard_map/ppermute | solution.py:637
  4.5 23.2 %collective-permute-start.7 = (bf16[64,2048]{1,0:T(8,128)(2,1)S(1)}, bf16[64,2048]{1,0:T(8,128)(2,1)S(1)}, u32[]{:S(2)}, u32[]{:S(2)}) collective-permute-start(bf16[64,2048]{1,0:T(8,128)(2,1)S(1)} %get-tuple-element.58), channel_id=1, source_target_pairs={{0,4},{4,8},{8,12},{12,14},{14,10},{10,6},{6,2},{2,0},{1,5},{5,9},... | collective-permute-start | bytes 786440 | tf_op jit(solution)/shard_map/ppermute | solution.py:637
  5.0 22.7 %collective-permute-start.8 = (bf16[64,2048]{1,0:T(8,128)(2,1)S(1)}, bf16[64,2048]{1,0:T(8,128)(2,1)S(1)}, u32[]{:S(2)}, u32[]{:S(2)}) collective-permute-start(bf16[64,2048]{1,0:T(8,128)(2,1)S(1)} %get-tuple-element.57), channel_id=1, source_target_pairs={{0,2},{4,0},{8,4},{12,8},{14,12},{10,14},{6,10},{2,6},{1,3},{5,1},... | collective-permute-start | bytes 786440 | tf_op jit(solution)/shard_map/ppermute | solution.py:637
  10.6 15.0 %collective-permute-start.2 = (bf16[256,256]{1,0:T(8,128)(2,1)S(1)}, bf16[256,256]{1,0:T(8,128)(2,1)S(1)}, u32[]{:S(2)}, u32[]{:S(2)}) collective-permute-start(bf16[256,256]{1,0:T(8,128)(2,1)S(1)} %collective-permute-done.refs_3_), channel_id=1, source_target_pairs={{0,4},{4,8},{8,12},{12,14},{14,10},{10,6},{6,2},{2,0},{1,5},{5,9},... | collective-permute-start | bytes 393224 | tf_op jit(solution)/shard_map/ppermute | solution.py:637
  11.1 14.5 %collective-permute-start.3 = (bf16[256,256]{1,0:T(8,128)(2,1)S(1)}, bf16[256,256]{1,0:T(8,128)(2,1)S(1)}, u32[]{:S(2)}, u32[]{:S(2)}) collective-permute-start(bf16[256,256]{1,0:T(8,128)(2,1)S(1)} %collective-permute-done.1.refs_4_), channel_id=1, source_target_pairs={{0,2},{4,0},{8,4},{12,8},{14,12},{10,14},{6,10},{2,6},{1,3},{5,1},... | collective-permute-start | bytes 393224 | tf_op jit(solution)/shard_map/ppermute | solution.py:637
  25.6 6.5 %collective-permute-start.4 = (bf16[256,256]{1,0:T(8,128)(2,1)S(1)}, bf16[256,256]{1,0:T(8,128)(2,1)S(1)}, u32[]{:S(2)}, u32[]{:S(2)}) collective-permute-start(bf16[256,256]{1,0:T(8,128)(2,1)S(1)} %collective-permute-done.2.refs_5_), channel_id=1, source_target_pairs={{0,4},{4,8},{8,12},{12,14},{14,10},{10,6},{6,2},{2,0},{1,5},{5,9},... | collective-permute-start | bytes 393224 | tf_op jit(solution)/shard_map/ppermute | solution.py:637
  26.1 6.4 %collective-permute-start.5 = (bf16[256,256]{1,0:T(8,128)(2,1)S(1)}, bf16[256,256]{1,0:T(8,128)(2,1)S(1)}, u32[]{:S(2)}, u32[]{:S(2)}) collective-permute-start(bf16[256,256]{1,0:T(8,128)(2,1)S(1)} %collective-permute-done.3.refs_6_), channel_id=1, source_target_pairs={{0,2},{4,0},{8,4},{12,8},{14,12},{10,14},{6,10},{2,6},{1,3},{5,1},... | collective-permute-start | bytes 393224 | tf_op jit(solution)/shard_map/ppermute | solution.py:637
  27.7 10.0 %collective-permute-start.9 = (bf16[64,2048]{1,0:T(8,128)(2,1)S(1)}, bf16[64,2048]{1,0:T(8,128)(2,1)S(1)}, u32[]{:S(2)}, u32[]{:S(2)}) collective-permute-start(bf16[64,2048]{1,0:T(8,128)(2,1)S(1)} %get-tuple-element.57), channel_id=1, source_target_pairs={{0,4},{4,8},{8,12},{12,14},{14,10},{10,6},{6,2},{2,0},{1,5},{5,9},... | collective-permute-start | bytes 786440 | tf_op jit(solution)/shard_map/ppermute | solution.py:637
  28.2 10.0 %collective-permute-start.10 = (bf16[64,2048]{1,0:T(8,128)(2,1)S(1)}, bf16[64,2048]{1,0:T(8,128)(2,1)S(1)}, u32[]{:S(2)}, u32[]{:S(2)}) collective-permute-start(bf16[64,2048]{1,0:T(8,128)(2,1)S(1)} %get-tuple-element.58), channel_id=1, source_target_pairs={{0,2},{4,0},{8,4},{12,8},{14,12},{10,14},{6,10},{2,6},{1,3},{5,1},... | collective-permute-start | bytes 786440 | tf_op jit(solution)/shard_map/ppermute | solution.py:637
  32.5 8.0 %collective-permute-start.6 = (bf16[256,256]{1,0:T(8,128)(2,1)S(1)}, bf16[256,256]{1,0:T(8,128)(2,1)S(1)}, u32[]{:S(2)}, u32[]{:S(2)}) collective-permute-start(bf16[256,256]{1,0:T(8,128)(2,1)S(1)} %collective-permute-done.4.refs_7_), channel_id=1, source_target_pairs={{0,4},{4,8},{8,12},{12,14},{14,10},{10,6},{6,2},{2,0},{1,5},{5,9},... | collective-permute-start | bytes 393224 | tf_op jit(solution)/shard_map/ppermute | solution.py:637
  32.6 19.7 %collective-permute-start.11 = (bf16[64,2048]{1,0:T(8,128)(2,1)S(1)}, bf16[64,2048]{1,0:T(8,128)(2,1)S(1)}, u32[]{:S(2)}, u32[]{:S(2)}) collective-permute-start(bf16[64,2048]{1,0:T(8,128)(2,1)S(1)} %collective-permute-done.7.refs_10_), channel_id=1, source_target_pairs={{0,4},{4,8},{8,12},{12,14},{14,10},{10,6},{6,2},{2,0},{1,5},{5,9},... | collective-permute-start | bytes 786440 | tf_op jit(solution)/shard_map/ppermute | solution.py:637
  32.6 19.7 %collective-permute-start.12 = (bf16[64,2048]{1,0:T(8,128)(2,1)S(1)}, bf16[64,2048]{1,0:T(8,128)(2,1)S(1)}, u32[]{:S(2)}, u32[]{:S(2)}) collective-permute-start(bf16[64,2048]{1,0:T(8,128)(2,1)S(1)} %collective-permute-done.8.refs_11_), channel_id=1, source_target_pairs={{0,2},{4,0},{8,4},{12,8},{14,12},{10,14},{6,10},{2,6},{1,3},{5,1},... | collective-permute-start | bytes 786440 | tf_op jit(solution)/shard_map/ppermute | solution.py:637
  38.1 34.9 %collective-permute-start.13 = (bf16[64,2048]{1,0:T(8,128)(2,1)S(1)}, bf16[64,2048]{1,0:T(8,128)(2,1)S(1)}, u32[]{:S(2)}, u32[]{:S(2)}) collective-permute-start(bf16[64,2048]{1,0:T(8,128)(2,1)S(1)} %collective-permute-done.9.refs_12_), channel_id=1, source_target_pairs={{0,4},{4,8},{8,12},{12,14},{14,10},{10,6},{6,2},{2,0},{1,5},{5,9},... | collective-permute-start | bytes 786440 | tf_op jit(solution)/shard_map/ppermute | solution.py:637
  38.2 34.9 %collective-permute-start.14 = (bf16[64,2048]{1,0:T(8,128)(2,1)S(1)}, bf16[64,2048]{1,0:T(8,128)(2,1)S(1)}, u32[]{:S(2)}, u32[]{:S(2)}) collective-permute-start(bf16[64,2048]{1,0:T(8,128)(2,1)S(1)} %collective-permute-done.10.refs_13_), channel_id=1, source_target_pairs={{0,2},{4,0},{8,4},{12,8},{14,12},{10,14},{6,10},{2,6},{1,3},{5,1},... | collective-permute-start | bytes 786440 | tf_op jit(solution)/shard_map/ppermute | solution.py:637
  52.3 41.7 %collective-permute-start.15 = (bf16[64,2048]{1,0:T(8,128)(2,1)S(1)}, bf16[64,2048]{1,0:T(8,128)(2,1)S(1)}, u32[]{:S(2)}, u32[]{:S(2)}) collective-permute-start(bf16[64,2048]{1,0:T(8,128)(2,1)S(1)} %collective-permute-done.11.refs_1_), channel_id=1, source_target_pairs={{0,4},{4,8},{8,12},{12,14},{14,10},{10,6},{6,2},{2,0},{1,5},{5,9},... | collective-permute-start | bytes 786440 | tf_op jit(solution)/shard_map/ppermute | solution.py:637
  52.4 41.7 %collective-permute-start.16 = (bf16[64,2048]{1,0:T(8,128)(2,1)S(1)}, bf16[64,2048]{1,0:T(8,128)(2,1)S(1)}, u32[]{:S(2)}, u32[]{:S(2)}) collective-permute-start(bf16[64,2048]{1,0:T(8,128)(2,1)S(1)} %collective-permute-done.12.refs_2_), channel_id=1, source_target_pairs={{0,2},{4,0},{8,4},{12,8},{14,12},{10,14},{6,10},{2,6},{1,3},{5,1},... | collective-permute-start | bytes 786440 | tf_op jit(solution)/shard_map/ppermute | solution.py:637
  73.1 43.4 %collective-permute-start.17 = (bf16[64,2048]{1,0:T(8,128)(2,1)S(1)}, bf16[64,2048]{1,0:T(8,128)(2,1)S(1)}, u32[]{:S(2)}, u32[]{:S(2)}) collective-permute-start(bf16[64,2048]{1,0:T(8,128)(2,1)S(1)} %collective-permute-done.13.refs_1_), channel_id=1, source_target_pairs={{0,4},{4,8},{8,12},{12,14},{14,10},{10,6},{6,2},{2,0},{1,5},{5,9},... | collective-permute-start | bytes 786440 | tf_op jit(solution)/shard_map/ppermute | solution.py:637
  73.1 43.3 %collective-permute-start.18 = (bf16[64,2048]{1,0:T(8,128)(2,1)S(1)}, bf16[64,2048]{1,0:T(8,128)(2,1)S(1)}, u32[]{:S(2)}, u32[]{:S(2)}) collective-permute-start(bf16[64,2048]{1,0:T(8,128)(2,1)S(1)} %collective-permute-done.14.refs_2_), channel_id=1, source_target_pairs={{0,2},{4,0},{8,4},{12,8},{14,12},{10,14},{6,10},{2,6},{1,3},{5,1},... | collective-permute-start | bytes 786440 | tf_op jit(solution)/shard_map/ppermute | solution.py:637
  94.1 42.7 %collective-permute-start.19 = (bf16[64,2048]{1,0:T(8,128)(2,1)S(1)}, bf16[64,2048]{1,0:T(8,128)(2,1)S(1)}, u32[]{:S(2)}, u32[]{:S(2)}) collective-permute-start(bf16[64,2048]{1,0:T(8,128)(2,1)S(1)} %collective-permute-done.15.refs_1_), channel_id=1, source_target_pairs={{0,4},{4,8},{8,12},{12,14},{14,10},{10,6},{6,2},{2,0},{1,5},{5,9},... | collective-permute-start | bytes 786440 | tf_op jit(solution)/shard_map/ppermute | solution.py:637
  94.1 42.7 %collective-permute-start.20 = (bf16[64,2048]{1,0:T(8,128)(2,1)S(1)}, bf16[64,2048]{1,0:T(8,128)(2,1)S(1)}, u32[]{:S(2)}, u32[]{:S(2)}) collective-permute-start(bf16[64,2048]{1,0:T(8,128)(2,1)S(1)} %collective-permute-done.16.refs_2_), channel_id=1, source_target_pairs={{0,2},{4,0},{8,4},{12,8},{14,12},{10,14},{6,10},{2,6},{1,3},{5,1},... | collective-permute-start | bytes 786440 | tf_op jit(solution)/shard_map/ppermute | solution.py:637
where the time goes:
time: 155 us
  Pallas kernels  122 us (79%)
  starting transfers between devices  20.7 us (13%)
  waiting for transfers between devices  10.4 us (7%)
    pallas_call x4, Pallas kernels, attend_later(): pl.pallas_call(lambda *refs: later_kernel(places, *refs), out_shape=jax.S...  78.1 us
    ppermute x21, starting transfers between devices, shift(): return lax.ppermute(block, 'replica', pairs)  20.7 us
    pallas_call x1, Pallas kernels, attend_last(): pl.pallas_call(lambda *refs: last_kernel(before, places, *refs), out_shap...  17.9 us
    pallas_call x1, Pallas kernels, attend_local(): pl.pallas_call(local_kernel, out_shape=jax.ShapeDtypeStruct((2 * SLOTS, S...  12.9 us
    pallas_call x1, Pallas kernels, attend_first(): pl.pallas_call(lambda *refs: first_kernel(kv_offsets, places, *refs), out...  11.8 us
    ppermute x21, waiting for transfers between devices, shift(): return lax.ppermute(block, 'replica', pairs)  10.4 us
  transfers between devices with their start and end apart: 21, of which 7 were waited for; matrix products, arithmetic and copies ran while one was open for 0% of the time, Pallas kernels for 66%

commit v1 on v0

--- a/solution.py
+++ b/solution.py
@@ -11,6 +11,7 @@
 HDIM = 128
 SPAN = 128
 SLOTS = 2
+LANES = 128
 MAXC = 8
 BLOCK = 4
 PART = 2
@@ -93,7 +94,17 @@
     wanted = chosen & (slot_prompt[None, :, 1] == mine) & (ring[:, None] > 0)
     spans = jnp.where(wanted, slot_span[None, :, 1] + 1, 0)
     whole = jnp.where(chosen & (ring[:, None] == 0), lengths[None, :] + 1, 0)
-    return jnp.sum(spans + whole, axis=1) - 1
+    table = jnp.sum(spans + whole, axis=1, keepdims=True) - 1
+    return jnp.broadcast_to(table, (replicas, LANES))
+
+
+def entry(meta_ref, n):
+    return jnp.max(meta_ref[n : n + 1, :])
+
+
+def entries(meta_ref, offsets):
+    found = {offset: entry(meta_ref, offset) for offset in dict.fromkeys(offsets)}
+    return [found[offset] for offset in offsets]
 
 
 def widen(v_ref, wide_ref):
@@ -165,10 +176,10 @@
     def add(block, carry):
         found = [scores(shared, block, BLOCK, False) for shared in heads]
         for shared in heads:
-            mixed[shared] += products(shared, block, BLOCK, found[shared])
+            before = jnp.where(block > 0, mixed[shared], 0.0)
+            mixed[shared] = before + products(shared, block, BLOCK, found[shared])
         return carry
 
-    mixed[...] = jnp.zeros_like(mixed)
     most = k_ref.shape[0] // SPAN
     if most > BLOCK:
         lax.fori_loop(0, blocks, add, 0)
@@ -178,7 +189,8 @@
         def _(spans=spans):
             found = [scores(shared, blocks, spans, True) for shared in heads]
             for shared in heads:
-                whole = mixed[shared] + products(shared, blocks, spans, found[shared])
+                before = jnp.where(blocks > 0, mixed[shared], 0.0)
+                whole = before + products(shared, blocks, spans, found[shared])
                 divide(whole, shared, o_ref, bounds)
 
 
@@ -365,8 +377,9 @@
     blocks, refs = refs[: len(kv_offsets)], refs[len(kv_offsets) :]
     q_refs, refs = refs[: len(places)], refs[len(places) :]
     local, o_k, o_v, k_buf, wide, out_buf, o_ref, v_buf, zeros, in_sems, out_sems, span_sems, *work = refs
-    live = meta_ref[0]
+    live = entry(meta_ref, 0)
     half = SPAN // 2
+    kv_dests = entries(meta_ref, kv_offsets)
 
     def fetches():
         yield None, own_k.at[:SPAN], k_buf.at[rows_of(0)]
@@ -406,8 +419,7 @@
             k_buf[rows_of(span), :] = jnp.zeros((SPAN, k_buf.shape[1]), k_buf.dtype)
             v_buf[rows_of(span), :] = jnp.zeros((SPAN, v_buf.shape[1]), v_buf.dtype)
 
-    for block, offset in zip(blocks, kv_offsets, strict=True):
-        dest = meta_ref[offset]
+    for block, dest in zip(blocks, kv_dests, strict=True):
 
         @pl.when(dest >= 0)
         def _(block=block, dest=dest):
@@ -419,7 +431,7 @@
     copy_v = pltpu.make_async_copy(v_buf, o_v, out_sems.at[1])
     copy_k.start()
     copy_v.start()
-    dests = [meta_ref[offset] for offset, _ in places]
+    dests = entries(meta_ref, [offset for offset, _ in places])
 
     @pl.when(live > 1)
     def _():
@@ -451,7 +463,7 @@
             jax.ShapeDtypeStruct((count, tall, width), keys.dtype),
             jax.ShapeDtypeStruct((rows, width), keys.dtype),
         ),
-        in_specs=[SMEM, ANY, ANY] + [VMEM] * (len(kv_blocks) + count + 1),
+        in_specs=[VMEM, ANY, ANY] + [VMEM] * (len(kv_blocks) + count + 1),
         out_specs=(ANY, ANY, VMEM, VMEM, VMEM, ANY),
         scratch_shapes=[
             pltpu.VMEM((rows, key_width), keys.dtype),
@@ -468,7 +480,7 @@
 
 def later_kernel(places, meta_ref, *refs):
     q_refs, (k_ref, wide_ref, out_buf, *work) = refs[: len(places)], refs[len(places) :]
-    dests = [meta_ref[offset] for offset, _ in places]
+    dests = entries(meta_ref, [offset for offset, _ in places])
 
     @pl.when(any_of(dests))
     def _():
@@ -483,7 +495,7 @@
     return pl.pallas_call(
         lambda *refs: later_kernel(places, *refs),
         out_shape=jax.ShapeDtypeStruct((count, tall, width), ordered_keys.dtype),
-        in_specs=[SMEM] + [VMEM] * (count + 2),
+        in_specs=[VMEM] * (count + 3),
         out_specs=VMEM,
         scratch_shapes=work_space(count, tall, width, ordered_keys.shape[1]),
         compiler_params=pltpu.CompilerParams(vmem_limit_bytes=VMEM_BYTES),
@@ -495,18 +507,21 @@
     results, refs = refs[: len(before)], refs[len(before) :]
     q_refs, refs = refs[: len(places)], refs[len(places) :]
     k_ref, wide_ref, _, o_ref, out_buf, sems, out_sems, *work = refs
+    known = {
+        offset: entry(meta_ref, offset) for its_places in before for offset, _ in its_places
+    }
 
     def each(act):
         for n, (result, its_places) in enumerate(zip(results, before, strict=True)):
             for j, (offset, start) in enumerate(its_places):
-                dest = meta_ref[offset]
+                dest = known[offset]
                 copy = pltpu.make_async_copy(
                     result.at[j], o_ref.at[half_of(jnp.maximum(dest, 0), start)], sems.at[n, j]
                 )
                 pl.when(dest >= 0)(getattr(copy, act))
 
     each("start")
-    dests = [meta_ref[offset] for offset, _ in places]
+    dests = entries(meta_ref, [offset for offset, _ in places])
 
     @pl.when(any_of(dests))
     def _():
@@ -525,7 +540,7 @@
     return pl.pallas_call(
         lambda *refs: last_kernel(before, places, *refs),
         out_shape=jax.ShapeDtypeStruct(attention.shape, attention.dtype),
-        in_specs=[SMEM] + [VMEM] * (len(results) + count + 2) + [ANY],
+        in_specs=[VMEM] * (len(results) + count + 3) + [ANY],
         out_specs=ANY,
         input_output_aliases={len(results) + count + 3: 0},
         scratch_shapes=[

time: 155 us -> 152 us (0.981)
  the two profiles are of different devices: /device:TPU:10 before, /device:TPU:6 now
where the time goes in v1:
time: 152 us
  Pallas kernels  119 us (78%)
  starting transfers between devices  20.8 us (14%)
  waiting for transfers between devices  10.5 us (7%)
    pallas_call x4, Pallas kernels, attend_later(): pl.pallas_call(lambda *refs: later_kernel(places, *refs), out_shape=jax.S...  79.3 us
    ppermute x21, starting transfers between devices, shift(): return lax.ppermute(block, 'replica', pairs)  20.8 us
    pallas_call x1, Pallas kernels, attend_last(): pl.pallas_call(lambda *refs: last_kernel(before, places, *refs), out_shap...  14.3 us
    pallas_call x1, Pallas kernels, attend_local(): pl.pallas_call(local_kernel, out_shape=jax.ShapeDtypeStruct((2 * SLOTS, S...  12.7 us
    pallas_call x1, Pallas kernels, attend_first(): pl.pallas_call(lambda *refs: first_kernel(kv_offsets, places, *refs), out...  11.3 us
    ppermute x21, waiting for transfers between devices, shift(): return lax.ppermute(block, 'replica', pairs)  10.5 us
  transfers between devices with their start and end apart: 21, of which 7 were waited for; matrix products, arithmetic and copies ran while one was open for 0% of the time, Pallas kernels for 68%

profile of v1, /device:TPU:6, one launch (start us, length us, event | category | flops | bytes accessed | tf_op | source)
XLA Modules:
  0.0 152.0 jit_solution(7655190170044567216)
XLA Ops:
  0.6 0.0 copy-start.3
  0.6 0.0 copy-start.2
  0.7 0.0 copy-start.1
  0.7 0.0 copy-start.4
  0.7 0.0 copy-start.5
  0.7 0.0 copy-start
  0.7 1.6 %shard_map.85 = bf16[256,256]{1,0:T(8,128)(2,1)} custom-call(bf16[256,256]{1,0:T(8,128)(2,1)} %refs_1_.1, bf16[256,256]{1,0:T(8,128)(2,1)} %refs_2_.1), custom_call_target="tpu_custom_call" | custom-call | flops 1150000000 | tf_op jit(solution)/shard_map/pallas_call | solution.py:52
  2.3 1.6 %collective-permute-start.1 = (bf16[256,256]{1,0:T(8,128)(2,1)}, bf16[256,256]{1,0:T(8,128)(2,1)S(1)}, u32[]{:S(2)}, u32[]{:S(2)}) collective-permute-start(bf16[256,256]{1,0:T(8,128)(2,1)} %shard_map.85), channel_id=1, source_target_pairs={{0,2},{4,0},{8,4},{12,8},{14,12},{10,14},{6,10},{2,6},{1,3},{5,1},... | collective-permute-start | bytes 393224 | tf_op jit(solution)/shard_map/ppermute | solution.py:652
  4.0 0.4 collective-permute-start
  4.4 0.0 copy-done.1
  4.4 0.1 shard_map.87
  4.5 0.6 collective-permute-start.7
  5.1 1.5 collective-permute-start.8
  6.6 0.0 copy-done.4
  6.6 0.0 copy-done.5
  6.6 0.0 copy-done
  6.6 2.3 %collective-permute-done.1.refs_4_ = bf16[256,256]{1,0:T(8,128)(2,1)S(1)} collective-permute-done((bf16[256,256]{1,0:T(8,128)(2,1)}, bf16[256,256]{1,0:T(8,128)(2,1)S(1)}, u32[]{:S(2)}, u32[]{:S(2)}) %collective-permute-start.1) | collective-permute-done | bytes 131104 | tf_op jit(solution)/shard_map/ppermute | solution.py:652
  9.0 1.6 %collective-permute-done.refs_3_ = bf16[256,256]{1,0:T(8,128)(2,1)S(1)} collective-permute-done((bf16[256,256]{1,0:T(8,128)(2,1)}, bf16[256,256]{1,0:T(8,128)(2,1)S(1)}, u32[]{:S(2)}, u32[]{:S(2)}) %collective-permute-start) | collective-permute-done | bytes 131104 | tf_op jit(solution)/shard_map/ppermute | solution.py:652
  10.6 0.4 collective-permute-start.2
  11.1 1.6 %collective-permute-start.3 = (bf16[256,256]{1,0:T(8,128)(2,1)S(1)}, bf16[256,256]{1,0:T(8,128)(2,1)S(1)}, u32[]{:S(2)}, u32[]{:S(2)}) collective-permute-start(bf16[256,256]{1,0:T(8,128)(2,1)S(1)} %collective-permute-done.1.refs_4_), channel_id=1, source_target_pairs={{0,2},{4,0},{8,4},{12,8},{14,12},{10,14},{6,10},{2,6},{1,3},{5,1},... | collective-permute-start | bytes 393224 | tf_op jit(solution)/shard_map/ppermute | solution.py:652
  12.6 0.0 copy-done.3
  12.6 12.7 %shard_map.86.refs_14_ = bf16[4,64,2048]{2,1,0:T(8,128)(2,1)S(1)} custom-call(s32[8]{0:T(128)S(1)} %copy-done, bf16[256,2048]{1,0:T(8,128)(2,1)S(1)} %copy-done.1, bf16[256,256]{1,0:T(8,128)(2,1)S(1)} %copy-done.2, bf16[256,256]{1,0:T(8,128)(2,1)S(1)} %copy-done.3), custom_call_target="tpu_custom_call" | custom-call | flops 4024999936 | tf_op jit(solution)/shard_map/pallas_call | solution.py:354
  25.4 0.0 collective-permute-done.2.refs_5_
  25.4 0.0 collective-permute-done.3.refs_6_
  25.4 0.1 collective-permute-start.4
  25.5 2.0 %collective-permute-start.5 = (bf16[256,256]{1,0:T(8,128)(2,1)S(1)}, bf16[256,256]{1,0:T(8,128)(2,1)S(1)}, u32[]{:S(2)}, u32[]{:S(2)}) collective-permute-start(bf16[256,256]{1,0:T(8,128)(2,1)S(1)} %collective-permute-done.3.refs_6_), channel_id=1, source_target_pairs={{0,2},{4,0},{8,4},{12,8},{14,12},{10,14},{6,10},{2,6},{1,3},{5,1},... | collective-permute-start | bytes 393224 | tf_op jit(solution)/shard_map/ppermute | solution.py:652
  27.5 0.0 collective-permute-done.7.refs_10_
  27.5 0.0 collective-permute-done.8.refs_11_
  27.5 0.1 collective-permute-start.9
  27.6 2.0 %collective-permute-start.10 = (bf16[64,2048]{1,0:T(8,128)(2,1)S(1)}, bf16[64,2048]{1,0:T(8,128)(2,1)S(1)}, u32[]{:S(2)}, u32[]{:S(2)}) collective-permute-start(bf16[64,2048]{1,0:T(8,128)(2,1)S(1)} %get-tuple-element.58), channel_id=1, source_target_pairs={{0,2},{4,0},{8,4},{12,8},{14,12},{10,14},{6,10},{2,6},{1,3},{5,1},... | collective-permute-start | bytes 786440 | tf_op jit(solution)/shard_map/ppermute | solution.py:652
  29.6 0.2 add_reduce_fusion
  29.7 2.1 %collective-permute-done.4.refs_7_ = bf16[256,256]{1,0:T(8,128)(2,1)S(1)} collective-permute-done((bf16[256,256]{1,0:T(8,128)(2,1)S(1)}, bf16[256,256]{1,0:T(8,128)(2,1)S(1)}, u32[]{:S(2)}, u32[]{:S(2)}) %collective-permute-start.4) | collective-permute-done | bytes 131104 | tf_op jit(solution)/shard_map/ppermute | solution.py:652
  31.9 0.1 collective-permute-done.5.refs_8_
  31.9 0.0 collective-permute-start.6
  31.9 0.0 collective-permute-start.11
  32.0 2.0 %collective-permute-start.12 = (bf16[64,2048]{1,0:T(8,128)(2,1)S(1)}, bf16[64,2048]{1,0:T(8,128)(2,1)S(1)}, u32[]{:S(2)}, u32[]{:S(2)}) collective-permute-start(bf16[64,2048]{1,0:T(8,128)(2,1)S(1)} %collective-permute-done.8.refs_11_), channel_id=1, source_target_pairs={{0,2},{4,0},{8,4},{12,8},{14,12},{10,14},{6,10},{2,6},{1,3},{5,1},... | collective-permute-start | bytes 786440 | tf_op jit(solution)/shard_map/ppermute | solution.py:652
  34.0 3.5 %collective-permute-done.9.refs_12_ = bf16[64,2048]{1,0:T(8,128)(2,1)S(1)} collective-permute-done((bf16[64,2048]{1,0:T(8,128)(2,1)S(1)}, bf16[64,2048]{1,0:T(8,128)(2,1)S(1)}, u32[]{:S(2)}, u32[]{:S(2)}) %collective-permute-start.9) | collective-permute-done | bytes 262176 | tf_op jit(solution)/shard_map/ppermute | solution.py:652
  37.5 0.1 collective-permute-done.10.refs_13_
  37.6 0.0 collective-permute-start.13
  37.6 2.0 %collective-permute-start.14 = (bf16[64,2048]{1,0:T(8,128)(2,1)S(1)}, bf16[64,2048]{1,0:T(8,128)(2,1)S(1)}, u32[]{:S(2)}, u32[]{:S(2)}) collective-permute-start(bf16[64,2048]{1,0:T(8,128)(2,1)S(1)} %collective-permute-done.10.refs_13_), channel_id=1, source_target_pairs={{0,2},{4,0},{8,4},{12,8},{14,12},{10,14},{6,10},{2,6},{1,3},{5,1},... | collective-permute-start | bytes 786440 | tf_op jit(solution)/shard_map/ppermute | solution.py:652
  39.6 0.7 collective-permute-done.6.refs_9_
  40.3 0.1 broadcast_in_dim.32.refs_0_
  40.4 11.3 %shard_map.88 = (bf16[1024,256]{1,0:T(8,128)(2,1)}, bf16[1024,256]{1,0:T(8,128)(2,1)}, bf16[1024,256]{1,0:T(8,128)(2,1)S(1)}, bf16[1024,512]{1,0:T(8,128)(2,1)S(...) custom-call(s32[8,128]{1,0:T(8,128)S(1)} %broadcast_in_dim.32.refs_0_, bf16[256,256]{1,0:T(8,128)(2,1)S(1)} %copy-done.2, ...), custom_call_target="tpu_custom_call" | custom-call | flops 8280000000 | tf_op jit(solution)/shard_map/pallas_call | solution.py:456
  51.7 0.0 collective-permute-done.11.refs_1_
  51.7 0.0 collective-permute-done.12.refs_2_
  51.7 0.1 collective-permute-start.15
  51.8 2.0 %collective-permute-start.16 = (bf16[64,2048]{1,0:T(8,128)(2,1)S(1)}, bf16[64,2048]{1,0:T(8,128)(2,1)S(1)}, u32[]{:S(2)}, u32[]{:S(2)}) collective-permute-start(bf16[64,2048]{1,0:T(8,128)(2,1)S(1)} %collective-permute-done.12.refs_2_), channel_id=1, source_target_pairs={{0,2},{4,0},{8,4},{12,8},{14,12},{10,14},{6,10},{2,6},{1,3},{5,1},... | collective-permute-start | bytes 786440 | tf_op jit(solution)/shard_map/ppermute | solution.py:652
  53.8 21.0 %shard_map.89.refs_2_ = bf16[2,64,2048]{2,1,0:T(8,128)(2,1)S(1)} custom-call(s32[8,128]{1,0:T(8,128)S(1)} %broadcast_in_dim.32.refs_0_, bf16[64,2048]{1,0:T(8,128)(2,1)S(1)} %collective-permute-done.11.refs_1_, bf16[64,2048]{1,0:T(8,128)(2,1)S(1)} %collective-permute-done.12.refs_2_, bf16[1024,256]{1,0:T(8,128)(2,1)S(1)} %get-tuple-element.66.refs_3_.refs_8_, ...), custom_call_target="tpu_custom_call" | custom-call | flops 4140000000 | tf_op jit(solution)/shard_map/pallas_call | solution.py:495
  74.9 0.0 collective-permute-done.13.refs_1_
  74.9 0.0 collective-permute-done.14.refs_2_
  74.9 0.1 collective-permute-start.17
  75.0 2.0 %collective-permute-start.18 = (bf16[64,2048]{1,0:T(8,128)(2,1)S(1)}, bf16[64,2048]{1,0:T(8,128)(2,1)S(1)}, u32[]{:S(2)}, u32[]{:S(2)}) collective-permute-start(bf16[64,2048]{1,0:T(8,128)(2,1)S(1)} %collective-permute-done.14.refs_2_), channel_id=1, source_target_pairs={{0,2},{4,0},{8,4},{12,8},{14,12},{10,14},{6,10},{2,6},{1,3},{5,1},... | collective-permute-start | bytes 786440 | tf_op jit(solution)/shard_map/ppermute | solution.py:652
  77.0 21.0 %shard_map.90.refs_3_ = bf16[2,64,2048]{2,1,0:T(8,128)(2,1)S(1)} custom-call(s32[8,128]{1,0:T(8,128)S(1)} %broadcast_in_dim.32.refs_0_, bf16[64,2048]{1,0:T(8,128)(2,1)S(1)} %collective-permute-done.13.refs_1_, bf16[64,2048]{1,0:T(8,128)(2,1)S(1)} %collective-permute-done.14.refs_2_, bf16[1024,256]{1,0:T(8,128)(2,1)S(1)} %get-tuple-element.66.refs_3_.refs_8_, ...), custom_call_target="tpu_custom_call" | custom-call | flops 4140000000 | tf_op jit(solution)/shard_map/pallas_call | solution.py:495
  98.0 0.0 collective-permute-done.15.refs_1_
  98.0 0.0 collective-permute-done.16.refs_2_
  98.0 0.2 collective-permute-start.19
  98.3 2.0 %collective-permute-start.20 = (bf16[64,2048]{1,0:T(8,128)(2,1)S(1)}, bf16[64,2048]{1,0:T(8,128)(2,1)S(1)}, u32[]{:S(2)}, u32[]{:S(2)}) collective-permute-start(bf16[64,2048]{1,0:T(8,128)(2,1)S(1)} %collective-permute-done.16.refs_2_), channel_id=1, source_target_pairs={{0,2},{4,0},{8,4},{12,8},{14,12},{10,14},{6,10},{2,6},{1,3},{5,1},... | collective-permute-start | bytes 786440 | tf_op jit(solution)/shard_map/ppermute | solution.py:652
  100.3 18.6 %shard_map.91.refs_4_ = bf16[2,64,2048]{2,1,0:T(8,128)(2,1)S(1)} custom-call(s32[8,128]{1,0:T(8,128)S(1)} %broadcast_in_dim.32.refs_0_, bf16[64,2048]{1,0:T(8,128)(2,1)S(1)} %collective-permute-done.15.refs_1_, bf16[64,2048]{1,0:T(8,128)(2,1)S(1)} %collective-permute-done.16.refs_2_, bf16[1024,256]{1,0:T(8,128)(2,1)S(1)} %get-tuple-element.66.refs_3_.refs_8_, ...), custom_call_target="tpu_custom_call" | custom-call | flops 4140000000 | tf_op jit(solution)/shard_map/pallas_call | solution.py:495
  118.9 0.0 collective-permute-done.17.refs_1_
  118.9 0.0 collective-permute-done.18.refs_2_
  119.0 18.6 %shard_map.92.refs_5_ = bf16[2,64,2048]{2,1,0:T(8,128)(2,1)S(1)} custom-call(s32[8,128]{1,0:T(8,128)S(1)} %broadcast_in_dim.32.refs_0_, bf16[64,2048]{1,0:T(8,128)(2,1)S(1)} %collective-permute-done.17.refs_1_, bf16[64,2048]{1,0:T(8,128)(2,1)S(1)} %collective-permute-done.18.refs_2_, bf16[1024,256]{1,0:T(8,128)(2,1)S(1)} %get-tuple-element.66.refs_3_.refs_8_, ...), custom_call_target="tpu_custom_call" | custom-call | flops 4140000000 | tf_op jit(solution)/shard_map/pallas_call | solution.py:495
  137.6 0.0 collective-permute-done.19.refs_6_
  137.6 0.0 collective-permute-done.20.refs_7_
  137.6 14.3 %shard_map.93 = bf16[1024,2048]{1,0:T(8,128)(2,1)} custom-call(s32[8,128]{1,0:T(8,128)S(1)} %broadcast_in_dim.32.refs_0_, bf16[4,64,2048]{2,1,0:T(8,128)(2,1)S(1)} %get-tuple-element.61.refs_1_, bf16[2,64,2048]{2,1,0:T(8,128)(2,1)S(1)} %shard_map.89.refs_2_, bf16[2,64,2048]{2,1,0:T(8,128)(2,1)S(1)} %shard_map.90.refs_3_, ...), custom_call_target="tpu_custom_call", output_to_operand_aliasing={{}: (10, {})} | custom-call | flops 4600000000 | tf_op jit(solution)/shard_map/pallas_call | solution.py:540
  (6 shorter events, 0.0 us)
Async XLA Ops:
  0.6 12.0 %copy-start.3 = (bf16[256,256]{1,0:T(8,128)(2,1)S(1)}, bf16[256,256]{1,0:T(8,128)(2,1)}, u32[]{:S(2)}) copy-start(bf16[256,256]{1,0:T(8,128)(2,1)} %refs_2_.1) | copy-start | bytes 393220
  0.6 12.0 %copy-start.2 = (bf16[256,256]{1,0:T(8,128)(2,1)S(1)}, bf16[256,256]{1,0:T(8,128)(2,1)}, u32[]{:S(2)}) copy-start(bf16[256,256]{1,0:T(8,128)(2,1)} %refs_1_.1) | copy-start | bytes 393220
  0.7 3.8 %copy-start.1 = (bf16[256,2048]{1,0:T(8,128)(2,1)S(1)}, bf16[256,2048]{1,0:T(8,128)(2,1)}, u32[]{:S(2)}) copy-start(bf16[256,2048]{1,0:T(8,128)(2,1)} %q_ref) | copy-start | bytes 3145732
  0.7 5.9 %copy-start.4 = (s32[8,2]{0,1:T(2,128)S(1)}, s32[8,2]{0,1:T(2,128)}, u32[]{:S(2)}) copy-start(s32[8,2]{0,1:T(2,128)} %param.10) | copy-start | bytes 196
  0.7 5.9 %copy-start.5 = (s32[8,2]{0,1:T(2,128)S(1)}, s32[8,2]{0,1:T(2,128)}, u32[]{:S(2)}) copy-start(s32[8,2]{0,1:T(2,128)} %param.11) | copy-start | bytes 196
  0.7 5.9 %copy-start = (s32[8]{0:T(128)S(1)}, s32[8]{0:T(128)}, u32[]{:S(2)}) copy-start(s32[8]{0:T(128)} %length_ref.1) | copy-start | bytes 100
  2.3 6.6 %collective-permute-start.1 = (bf16[256,256]{1,0:T(8,128)(2,1)}, bf16[256,256]{1,0:T(8,128)(2,1)S(1)}, u32[]{:S(2)}, u32[]{:S(2)}) collective-permute-start(bf16[256,256]{1,0:T(8,128)(2,1)} %shard_map.85), channel_id=1, source_target_pairs={{0,2},{4,0},{8,4},{12,8},{14,12},{10,14},{6,10},{2,6},{1,3},{5,1},... | collective-permute-start | bytes 393224 | tf_op jit(solution)/shard_map/ppermute | solution.py:652
  4.0 6.6 %collective-permute-start = (bf16[256,256]{1,0:T(8,128)(2,1)}, bf16[256,256]{1,0:T(8,128)(2,1)S(1)}, u32[]{:S(2)}, u32[]{:S(2)}) collective-permute-start(bf16[256,256]{1,0:T(8,128)(2,1)} %shard_map.85), channel_id=1, source_target_pairs={{0,4},{4,8},{8,12},{12,14},{14,10},{10,6},{6,2},{2,0},{1,5},{5,9},... | collective-permute-start | bytes 393224 | tf_op jit(solution)/shard_map/ppermute | solution.py:652
  4.5 23.0 %collective-permute-start.7 = (bf16[64,2048]{1,0:T(8,128)(2,1)S(1)}, bf16[64,2048]{1,0:T(8,128)(2,1)S(1)}, u32[]{:S(2)}, u32[]{:S(2)}) collective-permute-start(bf16[64,2048]{1,0:T(8,128)(2,1)S(1)} %get-tuple-element.58), channel_id=1, source_target_pairs={{0,4},{4,8},{8,12},{12,14},{14,10},{10,6},{6,2},{2,0},{1,5},{5,9},... | collective-permute-start | bytes 786440 | tf_op jit(solution)/shard_map/ppermute | solution.py:652
  5.1 22.4 %collective-permute-start.8 = (bf16[64,2048]{1,0:T(8,128)(2,1)S(1)}, bf16[64,2048]{1,0:T(8,128)(2,1)S(1)}, u32[]{:S(2)}, u32[]{:S(2)}) collective-permute-start(bf16[64,2048]{1,0:T(8,128)(2,1)S(1)} %get-tuple-element.57), channel_id=1, source_target_pairs={{0,2},{4,0},{8,4},{12,8},{14,12},{10,14},{6,10},{2,6},{1,3},{5,1},... | collective-permute-start | bytes 786440 | tf_op jit(solution)/shard_map/ppermute | solution.py:652
  10.6 14.8 %collective-permute-start.2 = (bf16[256,256]{1,0:T(8,128)(2,1)S(1)}, bf16[256,256]{1,0:T(8,128)(2,1)S(1)}, u32[]{:S(2)}, u32[]{:S(2)}) collective-permute-start(bf16[256,256]{1,0:T(8,128)(2,1)S(1)} %collective-permute-done.refs_3_), channel_id=1, source_target_pairs={{0,4},{4,8},{8,12},{12,14},{14,10},{10,6},{6,2},{2,0},{1,5},{5,9},... | collective-permute-start | bytes 393224 | tf_op jit(solution)/shard_map/ppermute | solution.py:652
  11.1 14.3 %collective-permute-start.3 = (bf16[256,256]{1,0:T(8,128)(2,1)S(1)}, bf16[256,256]{1,0:T(8,128)(2,1)S(1)}, u32[]{:S(2)}, u32[]{:S(2)}) collective-permute-start(bf16[256,256]{1,0:T(8,128)(2,1)S(1)} %collective-permute-done.1.refs_4_), channel_id=1, source_target_pairs={{0,2},{4,0},{8,4},{12,8},{14,12},{10,14},{6,10},{2,6},{1,3},{5,1},... | collective-permute-start | bytes 393224 | tf_op jit(solution)/shard_map/ppermute | solution.py:652
  25.4 6.5 %collective-permute-start.4 = (bf16[256,256]{1,0:T(8,128)(2,1)S(1)}, bf16[256,256]{1,0:T(8,128)(2,1)S(1)}, u32[]{:S(2)}, u32[]{:S(2)}) collective-permute-start(bf16[256,256]{1,0:T(8,128)(2,1)S(1)} %collective-permute-done.2.refs_5_), channel_id=1, source_target_pairs={{0,4},{4,8},{8,12},{12,14},{14,10},{10,6},{6,2},{2,0},{1,5},{5,9},... | collective-permute-start | bytes 393224 | tf_op jit(solution)/shard_map/ppermute | solution.py:652
  25.5 6.5 %collective-permute-start.5 = (bf16[256,256]{1,0:T(8,128)(2,1)S(1)}, bf16[256,256]{1,0:T(8,128)(2,1)S(1)}, u32[]{:S(2)}, u32[]{:S(2)}) collective-permute-start(bf16[256,256]{1,0:T(8,128)(2,1)S(1)} %collective-permute-done.3.refs_6_), channel_id=1, source_target_pairs={{0,2},{4,0},{8,4},{12,8},{14,12},{10,14},{6,10},{2,6},{1,3},{5,1},... | collective-permute-start | bytes 393224 | tf_op jit(solution)/shard_map/ppermute | solution.py:652
  27.5 10.0 %collective-permute-start.9 = (bf16[64,2048]{1,0:T(8,128)(2,1)S(1)}, bf16[64,2048]{1,0:T(8,128)(2,1)S(1)}, u32[]{:S(2)}, u32[]{:S(2)}) collective-permute-start(bf16[64,2048]{1,0:T(8,128)(2,1)S(1)} %get-tuple-element.57), channel_id=1, source_target_pairs={{0,4},{4,8},{8,12},{12,14},{14,10},{10,6},{6,2},{2,0},{1,5},{5,9},... | collective-permute-start | bytes 786440 | tf_op jit(solution)/shard_map/ppermute | solution.py:652
  27.6 10.0 %collective-permute-start.10 = (bf16[64,2048]{1,0:T(8,128)(2,1)S(1)}, bf16[64,2048]{1,0:T(8,128)(2,1)S(1)}, u32[]{:S(2)}, u32[]{:S(2)}) collective-permute-start(bf16[64,2048]{1,0:T(8,128)(2,1)S(1)} %get-tuple-element.58), channel_id=1, source_target_pairs={{0,2},{4,0},{8,4},{12,8},{14,12},{10,14},{6,10},{2,6},{1,3},{5,1},... | collective-permute-start | bytes 786440 | tf_op jit(solution)/shard_map/ppermute | solution.py:652
  31.9 8.4 %collective-permute-start.6 = (bf16[256,256]{1,0:T(8,128)(2,1)S(1)}, bf16[256,256]{1,0:T(8,128)(2,1)S(1)}, u32[]{:S(2)}, u32[]{:S(2)}) collective-permute-start(bf16[256,256]{1,0:T(8,128)(2,1)S(1)} %collective-permute-done.4.refs_7_), channel_id=1, source_target_pairs={{0,4},{4,8},{8,12},{12,14},{14,10},{10,6},{6,2},{2,0},{1,5},{5,9},... | collective-permute-start | bytes 393224 | tf_op jit(solution)/shard_map/ppermute | solution.py:652
  31.9 19.8 %collective-permute-start.11 = (bf16[64,2048]{1,0:T(8,128)(2,1)S(1)}, bf16[64,2048]{1,0:T(8,128)(2,1)S(1)}, u32[]{:S(2)}, u32[]{:S(2)}) collective-permute-start(bf16[64,2048]{1,0:T(8,128)(2,1)S(1)} %collective-permute-done.7.refs_10_), channel_id=1, source_target_pairs={{0,4},{4,8},{8,12},{12,14},{14,10},{10,6},{6,2},{2,0},{1,5},{5,9},... | collective-permute-start | bytes 786440 | tf_op jit(solution)/shard_map/ppermute | solution.py:652
  32.0 19.8 %collective-permute-start.12 = (bf16[64,2048]{1,0:T(8,128)(2,1)S(1)}, bf16[64,2048]{1,0:T(8,128)(2,1)S(1)}, u32[]{:S(2)}, u32[]{:S(2)}) collective-permute-start(bf16[64,2048]{1,0:T(8,128)(2,1)S(1)} %collective-permute-done.8.refs_11_), channel_id=1, source_target_pairs={{0,2},{4,0},{8,4},{12,8},{14,12},{10,14},{6,10},{2,6},{1,3},{5,1},... | collective-permute-start | bytes 786440 | tf_op jit(solution)/shard_map/ppermute | solution.py:652
  37.6 37.3 %collective-permute-start.13 = (bf16[64,2048]{1,0:T(8,128)(2,1)S(1)}, bf16[64,2048]{1,0:T(8,128)(2,1)S(1)}, u32[]{:S(2)}, u32[]{:S(2)}) collective-permute-start(bf16[64,2048]{1,0:T(8,128)(2,1)S(1)} %collective-permute-done.9.refs_12_), channel_id=1, source_target_pairs={{0,4},{4,8},{8,12},{12,14},{14,10},{10,6},{6,2},{2,0},{1,5},{5,9},... | collective-permute-start | bytes 786440 | tf_op jit(solution)/shard_map/ppermute | solution.py:652
  37.6 37.3 %collective-permute-start.14 = (bf16[64,2048]{1,0:T(8,128)(2,1)S(1)}, bf16[64,2048]{1,0:T(8,128)(2,1)S(1)}, u32[]{:S(2)}, u32[]{:S(2)}) collective-permute-start(bf16[64,2048]{1,0:T(8,128)(2,1)S(1)} %collective-permute-done.10.refs_13_), channel_id=1, source_target_pairs={{0,2},{4,0},{8,4},{12,8},{14,12},{10,14},{6,10},{2,6},{1,3},{5,1},... | collective-permute-start | bytes 786440 | tf_op jit(solution)/shard_map/ppermute | solution.py:652
  51.7 46.3 %collective-permute-start.15 = (bf16[64,2048]{1,0:T(8,128)(2,1)S(1)}, bf16[64,2048]{1,0:T(8,128)(2,1)S(1)}, u32[]{:S(2)}, u32[]{:S(2)}) collective-permute-start(bf16[64,2048]{1,0:T(8,128)(2,1)S(1)} %collective-permute-done.11.refs_1_), channel_id=1, source_target_pairs={{0,4},{4,8},{8,12},{12,14},{14,10},{10,6},{6,2},{2,0},{1,5},{5,9},... | collective-permute-start | bytes 786440 | tf_op jit(solution)/shard_map/ppermute | solution.py:652
  51.8 46.2 %collective-permute-start.16 = (bf16[64,2048]{1,0:T(8,128)(2,1)S(1)}, bf16[64,2048]{1,0:T(8,128)(2,1)S(1)}, u32[]{:S(2)}, u32[]{:S(2)}) collective-permute-start(bf16[64,2048]{1,0:T(8,128)(2,1)S(1)} %collective-permute-done.12.refs_2_), channel_id=1, source_target_pairs={{0,2},{4,0},{8,4},{12,8},{14,12},{10,14},{6,10},{2,6},{1,3},{5,1},... | collective-permute-start | bytes 786440 | tf_op jit(solution)/shard_map/ppermute | solution.py:652
  74.9 44.1 %collective-permute-start.17 = (bf16[64,2048]{1,0:T(8,128)(2,1)S(1)}, bf16[64,2048]{1,0:T(8,128)(2,1)S(1)}, u32[]{:S(2)}, u32[]{:S(2)}) collective-permute-start(bf16[64,2048]{1,0:T(8,128)(2,1)S(1)} %collective-permute-done.13.refs_1_), channel_id=1, source_target_pairs={{0,4},{4,8},{8,12},{12,14},{14,10},{10,6},{6,2},{2,0},{1,5},{5,9},... | collective-permute-start | bytes 786440 | tf_op jit(solution)/shard_map/ppermute | solution.py:652
  75.0 44.0 %collective-permute-start.18 = (bf16[64,2048]{1,0:T(8,128)(2,1)S(1)}, bf16[64,2048]{1,0:T(8,128)(2,1)S(1)}, u32[]{:S(2)}, u32[]{:S(2)}) collective-permute-start(bf16[64,2048]{1,0:T(8,128)(2,1)S(1)} %collective-permute-done.14.refs_2_), channel_id=1, source_target_pairs={{0,2},{4,0},{8,4},{12,8},{14,12},{10,14},{6,10},{2,6},{1,3},{5,1},... | collective-permute-start | bytes 786440 | tf_op jit(solution)/shard_map/ppermute | solution.py:652
  98.0 39.6 %collective-permute-start.19 = (bf16[64,2048]{1,0:T(8,128)(2,1)S(1)}, bf16[64,2048]{1,0:T(8,128)(2,1)S(1)}, u32[]{:S(2)}, u32[]{:S(2)}) collective-permute-start(bf16[64,2048]{1,0:T(8,128)(2,1)S(1)} %collective-permute-done.15.refs_1_), channel_id=1, source_target_pairs={{0,4},{4,8},{8,12},{12,14},{14,10},{10,6},{6,2},{2,0},{1,5},{5,9},... | collective-permute-start | bytes 786440 | tf_op jit(solution)/shard_map/ppermute | solution.py:652
  98.3 39.3 %collective-permute-start.20 = (bf16[64,2048]{1,0:T(8,128)(2,1)S(1)}, bf16[64,2048]{1,0:T(8,128)(2,1)S(1)}, u32[]{:S(2)}, u32[]{:S(2)}) collective-permute-start(bf16[64,2048]{1,0:T(8,128)(2,1)S(1)} %collective-permute-done.16.refs_2_), channel_id=1, source_target_pairs={{0,2},{4,0},{8,4},{12,8},{14,12},{10,14},{6,10},{2,6},{1,3},{5,1},... | collective-permute-start | bytes 786440 | tf_op jit(solution)/shard_map/ppermute | solution.py:652
